TPU v7x, 32 devices: a whole 2x2x4 slice. The times are simulated.
32 devices in a mesh: dp: 16 (over z, y, core), tensor: 2 (over x).
Axes of the slice: x: 2, y: 2, z: 4, core: 2. Of those that a mesh axis runs over, the one named last changes fastest.
Arguments:
- tokens: bfloat16 [24576, 640], P('dp'), may hold values from -6 to 6
- w_query: bfloat16 [640, 1024], P(None, 'tensor'), may hold values from -0.25 to 0.25
- w_key: bfloat16 [640, 256], replicated, may hold values from -0.25 to 0.25
- w_value: bfloat16 [640, 256], replicated, may hold values from -0.25 to 0.25
- w_output: bfloat16 [1024, 640], P('tensor'), may hold values from -0.1875 to 0.1875
- w_gate: bfloat16 [640, 2048], P(None, 'tensor'), may hold values from -0.25 to 0.25
- w_up: bfloat16 [640, 2048], P(None, 'tensor'), may hold values from -0.25 to 0.25
- w_down: bfloat16 [2048, 640], P('tensor'), may hold values from -0.125 to 0.125
- gain_input: float32 [640], replicated, may hold values from -0.4 to 0.6
- gain_query: float32 [256], replicated, may hold values from -0.4 to 0.6
- gain_key: float32 [256], replicated, may hold values from -0.4 to 0.6
- gain_post_attn: float32 [640], replicated, may hold values from -0.4 to 0.6
- gain_pre_ffn: float32 [640], replicated, may hold values from -0.4 to 0.6
- gain_post_ffn: float32 [640], replicated, may hold values from -0.4 to 0.6
- out_grad: bfloat16 [24576, 640], P('dp'), may hold values from -6 to 6
- lengths: int32 [24], replicated, may hold values from 1 to 1536, as said below
- holder: int32 [24], replicated, may hold values from 0 to 15
Outputs:
- layer_out: float32 [24576, 640], P('dp')
- tokens_grad: float32 [24576, 640], P('dp')
- grad_w_query: float32 [640, 1024], P(None, 'tensor')
- grad_w_key: float32 [640, 256], replicated
- grad_w_value: float32 [640, 256], replicated
- grad_w_output: float32 [1024, 640], P('tensor')
- grad_w_gate: float32 [640, 2048], P(None, 'tensor')
- grad_w_up: float32 [640, 2048], P(None, 'tensor')
- grad_w_down: float32 [2048, 640], P('tensor')
- grad_gain_input: float32 [640], replicated
- grad_gain_query: float32 [256], replicated
- grad_gain_key: float32 [256], replicated
- grad_gain_post_attn: float32 [640], replicated
- grad_gain_pre_ffn: float32 [640], replicated
- grad_gain_post_ffn: float32 [640], replicated
Inputs may be any that keep to these rules, and one draw needn't show every extreme that they name: The sequences of one index d of dp (holder = d) have lengths summing to at most 1536; one sequence has exactly 1536 tokens; an index of dp holds 0 to 3 sequences.
All inputs are finite; a program needn't handle non-finite values.
Results may differ from a plain program's by a relative error of at most 0.015.
Values sent between devices are 32-bit elements; how exact they have to be, the bound alone decides.
A program may use at most 192 MiB of HBM per device.

v0:
```python
import jax
import jax.numpy as jnp
from jax import lax
from jax.sharding import PartitionSpec as P

HD = 256


EPS = 1e-06
THETA = 1000000.0


def layout(lengths, holder, device, tok_rows):
    seq_count = lengths.shape[0]
    owned_mask = holder == device
    local_len = jnp.where(owned_mask, lengths, 0)
    starts = jnp.cumsum(local_len) - local_len
    row_ids = jnp.arange(tok_rows, dtype=jnp.int32)[:, None]
    inside = (
        owned_mask[None, :]
        & (row_ids >= starts[None, :])
        & (row_ids < (starts + local_len)[None, :])
    )
    inside_int = inside.astype(jnp.int32)
    segment = (
        jnp.sum(inside_int * (jnp.arange(seq_count, dtype=jnp.int32)[None, :] + 1), axis=1) - 1
    )
    position = jnp.sum(inside_int * (row_ids - starts[None, :]), axis=1)
    return (segment, position)


def rotary_tables(position):
    half_width = HD // 2
    frequency = THETA ** (-(2.0 * jnp.arange(half_width, dtype=jnp.float32)) / HD)
    angles = position.astype(jnp.float32)[:, None] * frequency[None, :]
    angles = jnp.concatenate([angles, angles], axis=1)
    return (jnp.cos(angles), jnp.sin(angles))


def rotate(vectors, cosine, sine):
    half_width = vectors.shape[-1] // 2
    turned = jnp.concatenate([-vectors[..., half_width:], vectors[..., :half_width]], axis=-1)
    return vectors * cosine + turned * sine


def unrotate(grads_in, cosine, sine):
    half_width = grads_in.shape[-1] // 2
    weighted = grads_in * sine
    turned = jnp.concatenate([weighted[..., half_width:], -weighted[..., :half_width]], axis=-1)
    return grads_in * cosine + turned


def norm_forward(vectors, scaling):
    inverse = lax.rsqrt(jnp.mean(vectors * vectors, axis=-1, keepdims=True) + EPS)
    plain = vectors * inverse
    return (plain * (1.0 + scaling), plain, inverse)


def norm_backward(grads_in, plain, inverse, scaling):
    scaled = grads_in * (1.0 + scaling)
    grads_out = inverse * (scaled - plain * jnp.mean(scaled * plain, axis=-1, keepdims=True))
    gain_grad = jnp.sum(grads_in * plain, axis=tuple(range(grads_in.ndim - 1)))
    return (grads_out, gain_grad)


def left_dot(first, second):
    return lax.dot_general(
        first, second, (((0,), (0,)), ((), ())), preferred_element_type=jnp.float32
    )


def right_dot(first, second):
    return lax.dot_general(
        first, second, (((1,), (1,)), ((), ())), preferred_element_type=jnp.float32
    )


def left_full(first, second):
    return lax.dot_general(
        first,
        second,
        (((0,), (0,)), ((), ())),
        precision=lax.Precision.HIGHEST,
        preferred_element_type=jnp.float32,
    )


def right_full(first, second):
    return lax.dot_general(
        first,
        second,
        (((1,), (1,)), ((), ())),
        precision=lax.Precision.HIGHEST,
        preferred_element_type=jnp.float32,
    )


def gelu_tanh(vectors):
    return jax.nn.gelu(vectors, approximate=True)


def block_scores(query_block, key_states, segment, first_row, score_scale):
    block_rows = query_block.shape[0]
    total_rows = key_states.shape[0]
    row_ids = first_row + jnp.arange(block_rows, dtype=jnp.int32)
    column_ids = jnp.arange(total_rows, dtype=jnp.int32)
    seg_rows = lax.dynamic_slice_in_dim(segment, first_row, block_rows)
    allowed = (seg_rows[:, None] == segment[None, :]) & (seg_rows[:, None] >= 0) & (
        column_ids[None, :] <= row_ids[:, None]
    ) | (column_ids[None, :] == row_ids[:, None])
    raw_scores = (
        jnp.einsum("qhd,kd->hqk", query_block, key_states, preferred_element_type=jnp.float32)
        * score_scale
    )
    return jnp.where(allowed[None, :, :], raw_scores, -1e30)


def local(
    tokens,
    w_query,
    w_key,
    w_value,
    w_output,
    w_gate,
    w_up,
    w_down,
    gain_input,
    gain_query,
    gain_key,
    gain_post_attn,
    gain_pre_ffn,
    gain_post_ffn,
    out_grad,
    lengths,
    holder,
):
    tok_rows = tokens.shape[0]
    local_heads = w_query.shape[1] // HD
    score_scale = HD ** (-0.5)
    device = lax.axis_index("dp")
    segment, position = layout(lengths, holder, device, tok_rows)
    cosine, sine = rotary_tables(position)
    block_rows = min(512, tok_rows)
    block_count = tok_rows // block_rows
    first_rows = jnp.arange(block_count, dtype=jnp.int32) * block_rows
    source = tokens.astype(jnp.float32)
    normed, normed_plain, normed_inverse = norm_forward(source, gain_input)
    normed_low = normed.astype(jnp.bfloat16)
    query_pre = jnp.dot(normed_low, w_query, preferred_element_type=jnp.float32).reshape(
        tok_rows, local_heads, HD
    )
    key_pre = jnp.dot(normed_low, w_key, preferred_element_type=jnp.float32)
    value_pre = jnp.dot(normed_low, w_value, preferred_element_type=jnp.float32)
    query_normed, query_plain, query_inverse = norm_forward(query_pre, gain_query)
    query_states = rotate(query_normed, cosine[:, None, :], sine[:, None, :]).astype(jnp.bfloat16)
    key_normed, key_plain, key_inverse = norm_forward(key_pre, gain_key)
    key_states = rotate(key_normed, cosine, sine).astype(jnp.bfloat16)
    value_states = value_pre.astype(jnp.bfloat16)
    query_blocks = query_states.reshape(block_count, block_rows, local_heads, HD)

    def forward_block(inputs):
        query_block, first_row = inputs
        scores = block_scores(query_block, key_states, segment, first_row, score_scale)
        row_max = jnp.max(scores, axis=-1, keepdims=True)
        exponent = jnp.exp(scores - row_max)
        row_total = jnp.sum(exponent, axis=-1, keepdims=True)
        attn_probs = exponent / row_total
        mixed_block = jnp.einsum(
            "hqk,kd->qhd",
            attn_probs.astype(jnp.bfloat16),
            value_states,
            preferred_element_type=jnp.float32,
        )
        return (mixed_block, (row_max + jnp.log(row_total))[..., 0])

    mixed_blocks, log_totals = lax.map(forward_block, (query_blocks, first_rows))
    mixed_heads = mixed_blocks.reshape(tok_rows, local_heads * HD).astype(jnp.bfloat16)
    branch = lax.psum(jnp.dot(mixed_heads, w_output, preferred_element_type=jnp.float32), "tensor")
    post_attn, post_attn_plain, post_attn_inverse = norm_forward(branch, gain_post_attn)
    middle = source + post_attn
    normed2, normed2_plain, normed2_inverse = norm_forward(middle, gain_pre_ffn)
    normed2_low = normed2.astype(jnp.bfloat16)
    gate_proj = jnp.dot(normed2_low, w_gate, preferred_element_type=jnp.float32)
    up_proj = jnp.dot(normed2_low, w_up, preferred_element_type=jnp.float32)
    activation, gelu_pull = jax.vjp(gelu_tanh, gate_proj)
    hidden = (activation * up_proj).astype(jnp.bfloat16)
    ffn_sum = lax.psum(jnp.dot(hidden, w_down, preferred_element_type=jnp.float32), "tensor")
    post_ffn, post_ffn_plain, post_ffn_inverse = norm_forward(ffn_sum, gain_post_ffn)
    layer_out = middle + post_ffn
    valid = (segment >= 0).astype(jnp.float32)[:, None]
    upstream = out_grad.astype(jnp.float32) * valid
    grad_ffn, grad_post_ffn = norm_backward(
        upstream, post_ffn_plain, post_ffn_inverse, gain_post_ffn
    )
    grad_ffn_low = grad_ffn.astype(jnp.bfloat16)
    grad_down = left_dot(hidden, grad_ffn_low)
    grad_hidden = right_dot(grad_ffn_low, w_down)
    grad_gate_low = gelu_pull(grad_hidden * up_proj)[0].astype(jnp.bfloat16)
    grad_up_low = (grad_hidden * activation).astype(jnp.bfloat16)
    grad_gate = left_dot(normed2_low, grad_gate_low)
    grad_up = left_dot(normed2_low, grad_up_low)
    grad_normed2 = lax.psum(
        right_dot(grad_gate_low, w_gate) + right_dot(grad_up_low, w_up), "tensor"
    )
    grad_pre_part, grad_pre_ffn = norm_backward(
        grad_normed2, normed2_plain, normed2_inverse, gain_pre_ffn
    )
    grad_middle = upstream + grad_pre_part
    grad_branch, grad_post_attn = norm_backward(
        grad_middle, post_attn_plain, post_attn_inverse, gain_post_attn
    )
    grad_branch_low = grad_branch.astype(jnp.bfloat16)
    grad_output = left_dot(mixed_heads, grad_branch_low)
    grad_mixed = (
        right_dot(grad_branch_low, w_output)
        .astype(jnp.bfloat16)
        .reshape(block_count, block_rows, local_heads, HD)
    )

    def backward_block(sums_carry, inputs):
        key_sum, value_sum = sums_carry
        query_block, mixed_grad_block, total_block, first_row = inputs
        scores = block_scores(query_block, key_states, segment, first_row, score_scale)
        attn_probs = jnp.exp(scores - total_block[..., None])
        grad_probs = jnp.einsum(
            "qhd,kd->hqk", mixed_grad_block, value_states, preferred_element_type=jnp.float32
        )
        grad_scores = (
            attn_probs
            * (grad_probs - jnp.sum(attn_probs * grad_probs, axis=-1, keepdims=True))
            * score_scale
        ).astype(jnp.bfloat16)
        query_grad_block = jnp.einsum(
            "hqk,kd->qhd", grad_scores, key_states, preferred_element_type=jnp.float32
        )
        key_sum = key_sum + jnp.einsum(
            "hqk,qhd->kd", grad_scores, query_block, preferred_element_type=jnp.float32
        )
        value_sum = value_sum + jnp.einsum(
            "hqk,qhd->kd",
            attn_probs.astype(jnp.bfloat16),
            mixed_grad_block,
            preferred_element_type=jnp.float32,
        )
        return ((key_sum, value_sum), query_grad_block)

    zeroes = jnp.zeros((tok_rows, HD), jnp.float32)
    (grad_keys_part, grad_values_part), query_grad_blocks = lax.scan(
        backward_block, (zeroes, zeroes), (query_blocks, grad_mixed, log_totals, first_rows)
    )
    grad_queries = query_grad_blocks.reshape(tok_rows, local_heads, HD)
    grad_query_pre, grad_gain_query_part = norm_backward(
        unrotate(grad_queries, cosine[:, None, :], sine[:, None, :]),
        query_plain,
        query_inverse,
        gain_query,
    )
    grad_query_low = grad_query_pre.astype(jnp.bfloat16).reshape(tok_rows, local_heads * HD)
    grad_query = left_dot(normed_low, grad_query_low)
    normed_wide = normed_low.astype(jnp.float32)
    w_key_wide = w_key.astype(jnp.float32)
    w_value_wide = w_value.astype(jnp.float32)
    grad_keys, grad_values, from_query, grad_gain_query = lax.psum(
        (
            grad_keys_part,
            grad_values_part,
            right_dot(grad_query_low, w_query),
            grad_gain_query_part,
        ),
        "tensor",
    )
    grad_key_pre, grad_gain_key_local = norm_backward(
        unrotate(grad_keys, cosine, sine), key_plain, key_inverse, gain_key
    )
    grad_key_local = left_full(normed_wide, grad_key_pre)
    grad_value_local = left_full(normed_wide, grad_values)
    grad_normed = (
        from_query + right_full(grad_key_pre, w_key_wide) + right_full(grad_values, w_value_wide)
    )
    grad_key, grad_value, grad_gain_key = lax.psum(
        (grad_key_local, grad_value_local, grad_gain_key_local), "dp"
    )
    grad_input_part, grad_gain_input = norm_backward(
        grad_normed, normed_plain, normed_inverse, gain_input
    )
    tokens_grad = grad_middle + grad_input_part
    all_summed = (
        lax.psum_scatter(grad_query, "dp", scatter_dimension=0, tiled=True),
        lax.psum_scatter(grad_output, "dp", scatter_dimension=0, tiled=True),
        lax.psum_scatter(grad_gate, "dp", scatter_dimension=0, tiled=True),
        lax.psum_scatter(grad_up, "dp", scatter_dimension=0, tiled=True),
        lax.psum_scatter(grad_down, "dp", scatter_dimension=0, tiled=True),
        lax.psum_scatter(grad_gain_input, "dp", scatter_dimension=0, tiled=True),
        lax.psum_scatter(grad_gain_query, "dp", scatter_dimension=0, tiled=True),
        lax.psum_scatter(grad_post_attn, "dp", scatter_dimension=0, tiled=True),
        lax.psum_scatter(grad_pre_ffn, "dp", scatter_dimension=0, tiled=True),
        lax.psum_scatter(grad_post_ffn, "dp", scatter_dimension=0, tiled=True),
    )
    all_full = (
        lax.all_gather(all_summed[0], "dp", axis=0, tiled=True),
        lax.all_gather(all_summed[1], "dp", axis=0, tiled=True),
        lax.all_gather(all_summed[2], "dp", axis=0, tiled=True),
        lax.all_gather(all_summed[3], "dp", axis=0, tiled=True),
        lax.all_gather(all_summed[4], "dp", axis=0, tiled=True),
        lax.all_gather(all_summed[5], "dp", axis=0, tiled=True),
        lax.all_gather(all_summed[6], "dp", axis=0, tiled=True),
        lax.all_gather(all_summed[7], "dp", axis=0, tiled=True),
        lax.all_gather(all_summed[8], "dp", axis=0, tiled=True),
        lax.all_gather(all_summed[9], "dp", axis=0, tiled=True),
    )
    return (
        layer_out,
        tokens_grad,
        all_full[0],
        grad_key,
        grad_value,
        all_full[1],
        all_full[2],
        all_full[3],
        all_full[4],
        all_full[5],
        all_full[6],
        grad_gain_key,
        all_full[7],
        all_full[8],
        all_full[9],
    )


def solution(mesh):
    return jax.shard_map(
        local,
        mesh=mesh,
        in_specs=(
            P("dp", None),
            P(None, "tensor"),
            P(),
            P(),
            P("tensor", None),
            P(None, "tensor"),
            P(None, "tensor"),
            P("tensor", None),
            P(),
            P(),
            P(),
            P(),
            P(),
            P(),
            P("dp", None),
            P(),
            P(),
        ),
        out_specs=(
            P("dp", None),
            P("dp", None),
            P(None, "tensor"),
            P(),
            P(),
            P("tensor", None),
            P(None, "tensor"),
            P(None, "tensor"),
            P("tensor", None),
            P(),
            P(),
            P(),
            P(),
            P(),
            P(),
        ),
        check_vma=False,
    )
```

profile of v0, /device:TPU:0, one launch (start us, length us, event | category | flops | bytes accessed | tf_op | source)
XLA Modules:
  0.0 1547.5 jit_solution(16992179626408646211)
XLA Ops:
  19.4 7.5 fusion.77
  29.2 8.6 fusion.75
  37.8 3.3 multiply_reduce_fusion.11
  42.4 3.5 copy.118
  45.9 3.5 copy.120
  56.7 5.1 reshape.476
  61.9 6.1 fusion.72
  69.3 39.3 %while.29 = (s32[]{:T(128)}, bf16[3,512,2,256]{3,1,2,0:T(8,128)(2,1)}, f32[3,2,512]{2,1,0:T(2,128)S(1)}, s32[3]{0:T(128)S(1)}, s32[1536]{0:T(1024)S(1)}, /*index...) while((s32[]{:T(128)}, ...), condition=%wide.region_9.10_spmd.clone, body=%wide.region_6.9_spmd.sunk.clone | while | flops 1634205696 | bytes 40944880 | solution.py:176
  113.2 3.3 fusion.100
  117.3 105.1 %all-reduce.20.cloned.1.call-done = f32[1536,640]{1,0:T(8,128)} async-done(((f32[1536,640]{1,0:T(8,128)}), f32[1536,640]{1,0:T(8,128)}) %all-reduce.20.cloned.1.call-update) | async-done | bytes 3932176 | tf_op jit(solution)/shard_map/psum | solution.py:178
  231.7 6.2 multiply_convert_fusion.1
  239.6 4.6 fusion.102
  244.9 102.4 %all-reduce.22.cloned.1.call-done = f32[1536,640]{1,0:T(8,128)} async-done(((f32[1536,640]{1,0:T(8,128)}), f32[1536,640]{1,0:T(8,128)}) %all-reduce.22.cloned.1.call-update) | async-done | bytes 3932176 | tf_op jit(solution)/shard_map/psum | solution.py:187
  357.9 7.0 multiply_convert_fusion
  367.7 4.8 convolution_add_fusion
  375.6 100.0 %all-reduce.24.cloned.1.call-done = f32[1536,640]{1,0:T(8,128)} async-done(((f32[1536,640]{1,0:T(8,128)}), f32[1536,640]{1,0:T(8,128)}) %all-reduce.24.cloned.1.call-update) | async-done | bytes 3932176 | tf_op jit(solution)/shard_map/psum | solution.py:202
  475.5 5.1 multiply_reduce_fusion.1
  481.1 5.3 multiply_reduce_fusion.2
  492.2 4.1 convolution_convert_fusion
  496.3 3.5 reshape.478
  499.8 116.4 %while.30 = (s32[]{:T(128)}, f32[1536,256]{1,0:T(8,128)}, f32[1536,256]{1,0:T(8,128)S(1)}, f32[3,512,2,256]{3,1,2,0:T(8,128)}, s32[3]{0:T(128)S(1)}, /*index=5*/...) while((s32[]{:T(128)}, f32[1536,256]{1,0:T(8,128)}, ...), condition=%wide.region_21.22_spmd.clone.clone, body=%wide.region_19.21_spmd.clone.sunk.clone | while | flops 4054849536 | bytes 115111200 | solution.py:248
  506.1 3.1 fusion.186
  511.9 3.6 fusion.187
  515.6 12.1 fusion.188
  527.7 10.6 fusion.190
  544.6 3.1 fusion.186
  550.4 3.6 fusion.187
  554.1 12.5 fusion.188
  566.6 10.6 fusion.190
  583.5 3.1 fusion.186
  589.3 3.6 fusion.187
  593.0 12.5 fusion.188
  605.5 10.7 fusion.190
  616.2 4.5 copy.132
  620.7 5.2 copy.142
  632.9 22.3 %multiply_reduce_fusion.9 = (f32[256]{0:T(256)S(1)}, f32[3,512,2]{2,1,0:T(8,128)S(1)}) fusion(f32[3,512,2,256]{3,2,1,0:T(2,128)S(1)} %copy-done.14, f32[3,512,2]{2,1,0:T(8,128)S(1)} %bitcast.271, f32[256]{0:T(256)S(1)} %broadcast_add_fusion.6, f32[3,512,2,128]{3,2,1,0:T(2,128)S(1)} %copy.137, f32[3,512,2,128]{3,2,1,0:T(2,128)S(1)} %copy.136, ...), kind=kLoop, calls=%fused_computation.124 | loop fusion | flops 7074560 | bytes 11036672 | tf_op jit(solution)/shard_map/reduce_sum | solution.py:62
  655.6 5.4 copy.147
  662.8 3.7 copy.134
  666.5 5.8 fusion.70
  676.4 6.7 fusion.108
  683.1 6.2 fusion.107
  689.4 6.2 fusion.106
  696.4 49.6 %reduce-scatter.6.cloned.1.call-done = f32[40,512]{1,0:T(8,128)} async-done(((f32[640,512]{1,0:T(8,128)}), f32[40,512]{1,0:T(8,128)}) %reduce-scatter.6.cloned.1.call-update) | async-done | bytes 81936 | tf_op jit(solution)/shard_map/reduce_scatter | solution.py:288
  746.1 67.4 %reduce-scatter.14.cloned.1.call-done = f32[64,640]{1,0:T(8,128)} async-done(((f32[1024,640]{1,0:T(8,128)}), f32[64,640]{1,0:T(8,128)}) %reduce-scatter.14.cloned.1.call-update) | async-done | bytes 163856 | tf_op jit(solution)/shard_map/reduce_scatter | solution.py:292
  813.6 67.7 %reduce-scatter.12.cloned.1.call-done = f32[40,1024]{1,0:T(8,128)} async-done(((f32[640,1024]{1,0:T(8,128)}), f32[40,1024]{1,0:T(8,128)}) %reduce-scatter.12.cloned.1.call-update) | async-done | bytes 163856 | tf_op jit(solution)/shard_map/reduce_scatter | solution.py:291
  881.3 67.6 %reduce-scatter.10.cloned.1.call-done = f32[40,1024]{1,0:T(8,128)} async-done(((f32[640,1024]{1,0:T(8,128)}), f32[40,1024]{1,0:T(8,128)}) %reduce-scatter.10.cloned.1.call-update) | async-done | bytes 163856 | tf_op jit(solution)/shard_map/reduce_scatter | solution.py:290
  952.0 4.7 fusion.104
  960.6 28.7 %all-gather.8.cloned.1.call-done = f32[512,640]{1,0:T(8,128)} async-done(((f32[32,640]{1,0:T(8,128)}), f32[512,640]{1,0:T(8,128)}) %all-gather.8.cloned.1.call-update) | async-done | bytes 1310736 | tf_op jit(solution)/shard_map/all_gather | solution.py:301
  989.4 40.0 %all-gather.6.cloned.1.call-done = f32[640,512]{1,0:T(8,128)} async-done(((f32[40,512]{1,0:T(8,128)}), f32[640,512]{1,0:T(8,128)}) %all-gather.6.cloned.1.call-update) | async-done | bytes 1310736 | tf_op jit(solution)/shard_map/all_gather | solution.py:300
  1029.4 44.6 %all-gather.14.cloned.1.call-done = f32[1024,640]{1,0:T(8,128)} async-done(((f32[64,640]{1,0:T(8,128)}), f32[1024,640]{1,0:T(8,128)}) %all-gather.14.cloned.1.call-update) | async-done | bytes 2621456 | tf_op jit(solution)/shard_map/all_gather | solution.py:304
  1074.0 44.3 %all-gather.12.cloned.1.call-done = f32[640,1024]{1,0:T(8,128)} async-done(((f32[40,1024]{1,0:T(8,128)}), f32[640,1024]{1,0:T(8,128)}) %all-gather.12.cloned.1.call-update) | async-done | bytes 2621456 | tf_op jit(solution)/shard_map/all_gather | solution.py:303
  1118.3 44.4 %all-gather.10.cloned.1.call-done = f32[640,1024]{1,0:T(8,128)} async-done(((f32[40,1024]{1,0:T(8,128)}), f32[640,1024]{1,0:T(8,128)}) %all-gather.10.cloned.1.call-update) | async-done | bytes 2621456 | tf_op jit(solution)/shard_map/all_gather | solution.py:302
  1162.7 172.9 %all-reduce.28.cloned.1.call-done = (f32[1536,640]{1,0:T(8,128)}, f32[1536,256]{0,1:T(8,128)}, f32[1536,256]{1,0:T(8,128)}) async-done(((f32[1536,640]{1,0:T(8,128)}, f32[1536,256]{0,1:T(8,128)}, f32[1536,256]{1,0:T(8,128)}), (f32[1536,640]{1,0:T(8,128)}, f32[1536,256]{0,1:T(8,128)}, f32[1536,256]{1,0:T(8,128)})) %all-reduce.28.cloned.1.call-update) | async-done | bytes 7077904 | tf_op jit(solution)/shard_map/psum | solution.py:263
  1335.6 6.3 fusion.82
  1342.1 6.7 multiply_reduce_fusion.12
  1348.8 3.8 fusion.85
  1352.6 5.9 fusion.86
  1358.5 3.5 fusion.87
  1362.0 8.8 fusion.65
  1370.8 61.2 %all-reduce.11 = (f32[640]{0:T(1024)S(1)}, f32[256]{0:T(256)S(1)}, f32[640]{0:T(1024)S(1)}, f32[640]{0:T(1024)S(1)}, f32[640]{0:T(1024)S(1)}) all-reduce(f32[640]{0:T(1024)S(1)} %get-tuple-element.261, f32[256]{0:T(256)S(1)} %get-tuple-element.257, ...), channel_id=7, replica_groups=mesh['dp'=16,'tensor'=2] {'dp'}, use_global_device_ids=true, to_apply=%region_36.37.clone | all-reduce | flops 2816 | bytes 22528
  1432.1 4.9 psum.80
  1437.9 58.1 %all-reduce.10 = (f32[640]{0:T(1024)}, f32[256]{0:T(256)}, f32[256]{0:T(256)}, f32[640]{0:T(1024)}, f32[640]{0:T(1024)}, /*index=5*/f32[640]{0:T(1024)}) all-reduce(f32[640]{0:T(1024)S(1)} %dynamic-slice_dynamic-update-slice_fusion.3, f32[256]{0:T(256)S(1)} %dynamic-update-slice.1, ...), channel_id=1, replica_groups=mesh['dp'=16,'tensor'=2] {'dp'}, use_global_device_ids=true, to_apply=%add | all-reduce | flops 3072 | bytes 24576
  1496.0 5.2 fusion.64
  1501.2 26.2 %all-reduce.26.cloned.1.call-done = (f32[640,256]{1,0:T(8,128)}, f32[640,256]{1,0:T(8,128)}) async-done(((f32[640,256]{1,0:T(8,128)}, f32[640,256]{1,0:T(8,128)}), (f32[640,256]{1,0:T(8,128)}, f32[640,256]{1,0:T(8,128)})) %all-reduce.26.cloned.1.call-update) | async-done | bytes 1310736 | tf_op jit(solution)/shard_map/psum | solution.py:280
  (351 shorter events, 150.6 us)
Async XLA Ops:
  7.2 232.4 %copy-start = (bf16[1024,640]{1,0:T(8,128)(2,1)S(1)}, bf16[1024,640]{1,0:T(8,128)(2,1)}, u32[]{:S(2)}) copy-start(bf16[1024,640]{1,0:T(8,128)(2,1)} %param.28) | copy-start | bytes 3932164
  7.2 7.3 copy-start.11
  7.2 5.5 copy-start.64
  7.2 5.5 copy-start.66
  7.2 215.1 %all-reduce.20.cloned.1.call-start = ((), (), s32[]{:S(2)}) async-start(), calls=%async_computation.5 | async-start | bytes 7864320 | tf_op jit(solution)/shard_map/psum | solution.py:178
  9.3 9.4 copy-start.57
  10.7 27.1 %copy-start.55 = (f32[640]{0:T(1024)}, f32[640]{0:T(1024)S(1)}, u32[]{:S(2)}) copy-start(f32[640]{0:T(1024)S(1)} %broadcast_add_fusion.4) | copy-start | bytes 7684
  12.7 25.1 %copy-start.53 = (f32[1536]{0:T(1024)}, f32[1536]{0:T(1024)S(1)}, u32[]{:S(2)}) copy-start(f32[1536]{0:T(1024)S(1)} %add_rsqrt_fusion.5) | copy-start | bytes 18436
  13.3 5.3 copy-start.25
  13.3 3.9 copy-start.46
  29.2 8.6 copy-start.44
  41.2 8.3 copy-start.51
  108.6 4.6 copy-start.41
  116.6 230.7 %all-reduce.22.cloned.1.call-start = ((), (), s32[]{:S(2)}) async-start(), calls=%async_computation.6 | async-start | bytes 7864320 | tf_op jit(solution)/shard_map/psum | solution.py:187
  222.3 3.3 copy-start.6
  226.7 5.0 copy-start.3
  231.7 6.2 copy-start.71
  244.2 105.7 %copy-start.21 = (bf16[1536,640]{1,0:T(8,128)(2,1)S(1)}, bf16[1536,640]{1,0:T(8,128)(2,1)}, u32[]{:S(2)}) copy-start(bf16[1536,640]{1,0:T(8,128)(2,1)} %param.35) | copy-start | bytes 5898244
  244.2 231.3 %all-reduce.24.cloned.1.call-start = ((), (), s32[]{:S(2)}) async-start(), calls=%async_computation.7 | async-start | bytes 7864320 | tf_op jit(solution)/shard_map/psum | solution.py:202
  350.5 5.0 slice-start
  350.5 5.0 slice-start.2
  352.8 3.4 slice-start.1
  352.8 5.1 slice-start.3
  355.6 9.3 copy-start.37
  357.9 7.0 copy-start.68
  372.5 323.2 %reduce-scatter.8.cloned.1.call-start = ((), (), s32[]{:S(2)}) async-start(), calls=%async_computation.10 | async-start | bytes 1392640 | tf_op jit(solution)/shard_map/reduce_scatter | solution.py:289
  475.5 5.1 copy-start.5
  475.5 5.6 copy-start.7
  515.6 12.1 copy-start.40
  554.1 12.5 copy-start.40
  593.0 12.5 copy-start.40
  616.2 4.5 copy-start.8
  625.9 120.1 %reduce-scatter.6.cloned.1.call-start = ((), (), s32[]{:S(2)}) async-start(), calls=%async_computation.8 | async-start | bytes 1392640 | tf_op jit(solution)/shard_map/reduce_scatter | solution.py:288
  629.0 3.9 copy-start.14
  655.6 5.4 copy-start.23
  662.8 3.7 copy-start.52
  666.5 7.0 copy-start.12
  666.5 7.0 copy-start.54
  666.5 7.0 copy-start.56
  676.1 137.4 %reduce-scatter.14.cloned.1.call-start = ((), (), s32[]{:S(2)}) async-start(), calls=%async_computation.16 | async-start | bytes 2785280 | tf_op jit(solution)/shard_map/reduce_scatter | solution.py:292
  683.0 198.2 %reduce-scatter.12.cloned.1.call-start = ((), (), s32[]{:S(2)}) async-start(), calls=%async_computation.14 | async-start | bytes 2785280 | tf_op jit(solution)/shard_map/reduce_scatter | solution.py:291
  689.3 259.6 %reduce-scatter.10.cloned.1.call-start = ((), (), s32[]{:S(2)}) async-start(), calls=%async_computation.12 | async-start | bytes 2785280 | tf_op jit(solution)/shard_map/reduce_scatter | solution.py:290
  695.6 256.4 %copy-start.45 = (bf16[640,512]{1,0:T(8,128)(2,1)S(1)}, bf16[640,512]{1,0:T(8,128)(2,1)}, u32[]{:S(2)}) copy-start(bf16[640,512]{1,0:T(8,128)(2,1)} %param.22) | copy-start | bytes 1966084
  695.6 293.7 %all-gather.8.cloned.1.call-start = ((), (), s32[]{:S(2)}) async-start(), calls=%async_computation.11 | async-start | bytes 1392640 | tf_op jit(solution)/shard_map/all_gather | solution.py:301
  696.4 333.0 %all-gather.6.cloned.1.call-start = ((), (), s32[]{:S(2)}) async-start(), calls=%async_computation.9 | async-start | bytes 1392640 | tf_op jit(solution)/shard_map/all_gather | solution.py:300
  746.0 328.0 %all-gather.14.cloned.1.call-start = ((), (), s32[]{:S(2)}) async-start(), calls=%async_computation.17 | async-start | bytes 2785280 | tf_op jit(solution)/shard_map/all_gather | solution.py:304
  813.5 304.8 %all-gather.12.cloned.1.call-start = ((), (), s32[]{:S(2)}) async-start(), calls=%async_computation.15 | async-start | bytes 2785280 | tf_op jit(solution)/shard_map/all_gather | solution.py:303
  881.2 281.5 %all-gather.10.cloned.1.call-start = ((), (), s32[]{:S(2)}) async-start(), calls=%async_computation.13 | async-start | bytes 2785280 | tf_op jit(solution)/shard_map/all_gather | solution.py:302
  949.0 386.6 %all-reduce.28.cloned.1.call-start = ((), (), s32[]{:S(2)}) async-start(), calls=%async_computation.19 | async-start | bytes 14155776 | tf_op jit(solution)/shard_map/psum | solution.py:263
  956.8 378.8 %copy-start.26 = (f32[1536,128]{0,1:T(8,128)S(1)}, f32[1536,128]{0,1:T(8,128)}, u32[]{:S(2)}) copy-start(f32[1536,128]{0,1:T(8,128)} %copy-done.25) | copy-start | bytes 2359300
  956.8 570.6 %all-reduce.26.cloned.1.call-start = ((), (), s32[]{:S(2)}) async-start(), calls=%async_computation.18 | async-start | bytes 2621440 | tf_op jit(solution)/shard_map/psum | solution.py:280
  1335.6 6.4 copy-start.16
  1335.6 6.5 copy-start.32
  1335.6 6.5 copy-start.50
  1335.6 6.5 copy-start.58
  1348.8 3.8 copy-start.47
  1352.6 5.9 copy-start.38
  1358.5 3.5 copy-start.48
  1362.0 8.8 copy-start.59
  1362.0 8.8 copy-start.60
  1501.2 31.7 %copy-start.39 = (f32[512,640]{1,0:T(8,128)S(1)}, f32[512,640]{1,0:T(8,128)}, u32[]{:S(2)}) copy-start(f32[512,640]{1,0:T(8,128)} %all-gather.8.cloned.1.call-done) | copy-start | bytes 3932164
  1527.4 4.7 copy-start.43
  1529.9 4.0 copy-start.35
  1536.6 4.2 copy-start.1
  (42 other events, 87.4 us)
Sparse Core Ops, SparseCore 0:
  116.7 105.5 all-reduce.19
  244.3 102.8 all-reduce.21
  372.6 102.8 all-reduce.23
  626.0 58.4 reduce-scatter.7
  688.5 57.4 reduce-scatter.5
  750.6 62.8 reduce-scatter.13
  818.3 62.8 reduce-scatter.11
  886.0 62.8 reduce-scatter.9
  951.5 37.8 all-gather.7
  991.7 37.6 all-gather.5
  1031.9 42.0 all-gather.13
  1076.4 41.8 all-gather.11
  1120.8 41.8 all-gather.9
  1166.0 169.5 all-reduce.27
  1437.1 90.2 all-reduce.25
where the time goes:
time: 1550 us
  waiting for transfers between devices  962 us (62%)
  matrix products  203 us (13%)
  other arithmetic  126 us (8%)
  blocking collectives  124 us (8%)
  local copies, waits for them, and re-layouts  101 us (7%)
  between operations  17.6 us (1%)
    psum x1, waiting for transfers between devices, local(): lax.psum((grad_keys_part, grad_values_part, right_dot(grad_query_low, w_q...  173 us
    unnamed x2, blocking collectives  119 us
    psum x1, waiting for transfers between devices, local(): lax.psum(jnp.dot(mixed_heads, w_output, preferred_element_type=jnp.float3...  105 us
    psum x1, waiting for transfers between devices, local(): lax.psum(jnp.dot(hidden, w_down, preferred_element_type=jnp.float32), 'te...  102 us
    psum x1, waiting for transfers between devices, local(): lax.psum(right_dot(grad_gate_low, w_gate) + right_dot(grad_up_low, w_up),...  100 us
    reduce_scatter x1, waiting for transfers between devices, local(): lax.psum_scatter(grad_up, 'dp', scatter_dimension=0, tiled=True)  67.7 us
    reduce_scatter x1, waiting for transfers between devices, local(): lax.psum_scatter(grad_gate, 'dp', scatter_dimension=0, tiled=True)  67.6 us
    reduce_scatter x1, waiting for transfers between devices, local(): lax.psum_scatter(grad_down, 'dp', scatter_dimension=0, tiled=True)  67.4 us
  transfers between devices with their start and end apart: 15, of which 14 were waited for; matrix products, arithmetic and copies ran while one was open for 5% of the time, Pallas kernels for 0%

commit v1 on v0

v1 whole, which is shorter than its diff:
```python
import jax
import jax.numpy as jnp
from jax import lax
from jax.experimental import pallas as pl
from jax.experimental.pallas import tpu as pltpu
from jax.sharding import PartitionSpec as P

HD = 256


EPS = 1e-06
THETA = 1000000.0


def layout(lengths, holder, device, tok_rows):
    seq_count = lengths.shape[0]
    owned_mask = holder == device
    local_len = jnp.where(owned_mask, lengths, 0)
    ids = jnp.arange(seq_count, dtype=jnp.int32)
    starts = jnp.sum(jnp.where(ids[:, None] < ids[None, :], local_len[:, None], 0), axis=0)
    row_ids = jnp.arange(tok_rows, dtype=jnp.int32)[:, None]
    inside = (
        owned_mask[None, :]
        & (row_ids >= starts[None, :])
        & (row_ids < (starts + local_len)[None, :])
    )
    reached = jnp.sum(jnp.where(inside, row_ids - starts[None, :] + 1, 0), axis=1)
    return (reached > 0, jnp.maximum(reached - 1, 0))


def rotary_tables(position):
    half_width = HD // 2
    frequency = THETA ** (-(2.0 * jnp.arange(half_width, dtype=jnp.float32)) / HD)
    angles = position.astype(jnp.float32)[:, None] * frequency[None, :]
    return (jnp.cos(angles), jnp.sin(angles))


def rotate(vectors, cosine, sine):
    half_width = HD // 2
    first, second = vectors[:, :half_width], vectors[:, half_width:]
    return jnp.concatenate(
        [first * cosine - second * sine, second * cosine + first * sine], axis=1
    )


def unrotate(grads_in, cosine, sine):
    half_width = HD // 2
    first, second = grads_in[:, :half_width], grads_in[:, half_width:]
    return jnp.concatenate(
        [first * cosine + second * sine, second * cosine - first * sine], axis=1
    )


def norm_forward(vectors, scaling):
    inverse = lax.rsqrt(jnp.mean(vectors * vectors, axis=-1, keepdims=True) + EPS)
    plain = vectors * inverse
    return (plain * (1.0 + scaling), plain, inverse)


def norm_backward(grads_in, plain, inverse, scaling):
    scaled = grads_in * (1.0 + scaling)
    grads_out = inverse * (scaled - plain * jnp.mean(scaled * plain, axis=-1, keepdims=True))
    gain_grad = jnp.sum(grads_in * plain, axis=0)
    return (grads_out, gain_grad)


def dot(first, second):
    return jnp.dot(first, second, preferred_element_type=jnp.float32)


def left_dot(first, second):
    return lax.dot_general(
        first, second, (((0,), (0,)), ((), ())), preferred_element_type=jnp.float32
    )


def right_dot(first, second):
    return lax.dot_general(
        first, second, (((1,), (1,)), ((), ())), preferred_element_type=jnp.float32
    )


def gelu_tanh(vectors):
    return jax.nn.gelu(vectors, approximate=True)


def softmax_rows(row_ref, low_ref, query, keys):
    scores = right_dot(query, keys) * (HD ** (-0.5))
    column_ids = lax.broadcasted_iota(jnp.int32, scores.shape, 1)
    allowed = (column_ids <= row_ref[...]) & (column_ids >= low_ref[...])
    scores = jnp.where(allowed, scores, -1e30)
    exponent = jnp.exp(scores - jnp.max(scores, axis=1, keepdims=True))
    return exponent * (1.0 / jnp.sum(exponent, axis=1, keepdims=True))


def attend_kernel(row_ref, low_ref, query_ref, key_ref, value_ref, mixed_ref):
    probs = softmax_rows(row_ref, low_ref, query_ref[...], key_ref[...])
    mixed_ref[...] = dot(probs.astype(jnp.bfloat16), value_ref[...]).astype(jnp.bfloat16)


def attend_back_kernel(
    row_ref, low_ref, query_ref, key_ref, value_ref, grad_ref, query_grad_ref, key_sum, value_sum
):
    @pl.when(pl.program_id(0) == 0)
    def _():
        key_sum[...] = jnp.zeros_like(key_sum)
        value_sum[...] = jnp.zeros_like(value_sum)

    query, keys, grads_in = query_ref[...], key_ref[...], grad_ref[...]
    probs = softmax_rows(row_ref, low_ref, query, keys)
    value_sum[...] += left_dot(probs.astype(jnp.bfloat16), grads_in)
    grad_probs = right_dot(grads_in, value_ref[...])
    inner = jnp.sum(probs * grad_probs, axis=1, keepdims=True)
    grad_scores = (probs * (grad_probs - inner) * (HD ** (-0.5))).astype(jnp.bfloat16)
    query_grad_ref[...] = dot(grad_scores, keys)
    key_sum[...] += left_dot(grad_scores, query)


def attention_specs(block_rows, key_rows):
    column = pl.BlockSpec((block_rows, 1), lambda h: (0, 0))
    head = pl.BlockSpec((block_rows, HD), lambda h: (0, h))
    keys = pl.BlockSpec((key_rows, HD), lambda h: (0, 0))
    return column, head, keys


def attend(rows, lows, queries, keys, values, key_rows):
    block_rows, width = queries.shape
    heads = width // HD
    column, head, whole = attention_specs(block_rows, key_rows)
    work = block_rows * key_rows * heads
    return pl.pallas_call(
        attend_kernel,
        grid=(heads,),
        out_shape=jax.ShapeDtypeStruct(queries.shape, jnp.bfloat16),
        in_specs=[column, column, head, whole, whole],
        out_specs=head,
        compiler_params=pltpu.CompilerParams(vmem_limit_bytes=40 * 2**20),
        cost_estimate=pl.CostEstimate(
            flops=4 * work * HD, bytes_accessed=4 * 2**20, transcendentals=work
        ),
    )(rows, lows, queries, keys, values)


def attend_back(rows, lows, queries, keys, values, grads_in, key_rows):
    block_rows, width = queries.shape
    heads = width // HD
    column, head, whole = attention_specs(block_rows, key_rows)
    work = block_rows * key_rows * heads
    sums = jax.ShapeDtypeStruct((key_rows, HD), jnp.float32)
    return pl.pallas_call(
        attend_back_kernel,
        grid=(heads,),
        out_shape=(jax.ShapeDtypeStruct(queries.shape, jnp.float32), sums, sums),
        in_specs=[column, column, head, whole, whole, head],
        out_specs=(head, whole, whole),
        compiler_params=pltpu.CompilerParams(vmem_limit_bytes=48 * 2**20),
        cost_estimate=pl.CostEstimate(
            flops=10 * work * HD, bytes_accessed=8 * 2**20, transcendentals=work
        ),
    )(rows, lows, queries, keys, values, grads_in)


def across(array):
    return lax.ppermute(array, "tensor", [(0, 1), (1, 0)])


def swap(array, mask):
    size = lax.axis_size("dp")
    return lax.ppermute(array, "dp", [(i, i ^ mask) for i in range(size)])


def bit_of(mask):
    return (lax.axis_index("dp") // mask) % 2


def halve(array, mask):
    half = array.shape[0] // 2
    bit = bit_of(mask)
    sent = lax.dynamic_slice_in_dim(array, (1 - bit) * half, half)
    kept = lax.dynamic_slice_in_dim(array, bit * half, half)
    return kept + swap(sent, mask)


def join(array, mask):
    other = swap(array, mask)
    return jnp.where(
        bit_of(mask) == 0,
        jnp.concatenate([array, other], axis=0),
        jnp.concatenate([other, array], axis=0),
    )


def outer_masks():
    size = lax.axis_size("dp")
    masks, mask = [], 2
    while mask < size:
        masks.append(mask)
        mask *= 2
    return masks


def scatter_sum(mine, theirs):
    crossing = across(halve(theirs, 1))
    total = halve(mine, 1) + crossing
    for mask in outer_masks():
        total = halve(total, mask)
    return total


def spread(total):
    for mask in reversed(outer_masks()):
        total = join(total, mask)
    return join(total, 1)


def fetch(weight, one):
    half = weight.shape[0] // 2
    part = lax.dynamic_slice_in_dim(weight, bit_of(1) * half, half).astype(jnp.float32)
    theirs = join(across(part * one), 1)
    return (theirs * one).astype(jnp.bfloat16)


def local(
    tokens,
    w_query,
    w_key,
    w_value,
    w_output,
    w_gate,
    w_up,
    w_down,
    gain_input,
    gain_query,
    gain_key,
    gain_post_attn,
    gain_pre_ffn,
    gain_post_ffn,
    out_grad,
    lengths,
    holder,
):
    tok_rows, width = tokens.shape
    quarter = tok_rows // 4
    half_rows = tok_rows // 2
    device = lax.axis_index("dp")
    side = lax.axis_index("tensor")
    early, late = side * quarter, (3 - side) * quarter

    def own(array):
        return jnp.concatenate(
            [
                lax.dynamic_slice_in_dim(array, early, quarter),
                lax.dynamic_slice_in_dim(array, late, quarter),
            ],
            axis=0,
        )

    def others(array):
        return jnp.concatenate(
            [
                lax.dynamic_slice_in_dim(array, (1 - side) * quarter, quarter),
                lax.dynamic_slice_in_dim(array, (2 + side) * quarter, quarter),
            ],
            axis=0,
        )

    def whole_rows(mine):
        theirs = across(mine)
        return jnp.where(
            side == 0,
            jnp.concatenate([mine[:quarter], theirs, mine[quarter:]], axis=0),
            jnp.concatenate([theirs[:quarter], mine, theirs[quarter:]], axis=0),
        )

    one = (lengths[0] > 0).astype(jnp.float32)
    query_theirs = fetch(w_query, one)
    output_theirs = fetch(w_output, one)
    gate_theirs = fetch(w_gate, one)
    up_theirs = fetch(w_up, one)
    down_theirs = fetch(w_down, one)

    used, position = layout(lengths, holder, device, tok_rows)
    cosine, sine = rotary_tables(position)
    row_ids = jnp.arange(tok_rows, dtype=jnp.int32)
    rows = own(row_ids[:, None])
    lows = own((row_ids - position)[:, None])
    cosine_own, sine_own = own(cosine), own(sine)
    valid = own(used.astype(jnp.float32)[:, None])

    normed_all = norm_forward(tokens.astype(jnp.float32), gain_input)[0].astype(jnp.bfloat16)
    key_pre = dot(normed_all, w_key)
    value_states = dot(normed_all, w_value).astype(jnp.bfloat16)
    key_states = rotate(norm_forward(key_pre, gain_key)[0], cosine, sine).astype(jnp.bfloat16)
    _, key_plain, key_inverse = norm_forward(own(key_pre), gain_key)

    source = own(tokens).astype(jnp.float32)
    normed, normed_plain, normed_inverse = norm_forward(source, gain_input)
    normed_low = normed.astype(jnp.bfloat16)
    w_query_all = jnp.concatenate([w_query, query_theirs], axis=1)
    heads = w_query_all.shape[1] // HD
    query_pre = dot(normed_low, w_query_all)
    query_parts, query_norms = [], []
    for h in range(heads):
        out, plain, inverse = norm_forward(query_pre[:, h * HD : (h + 1) * HD], gain_query)
        query_norms.append((plain, inverse))
        query_parts.append(rotate(out, cosine_own, sine_own).astype(jnp.bfloat16))
    queries = jnp.concatenate(query_parts, axis=1)
    spans = ((slice(0, quarter), half_rows), (slice(quarter, half_rows), tok_rows))
    mixed = jnp.concatenate(
        [
            attend(rows[s], lows[s], queries[s], key_states, value_states, key_rows)
            for s, key_rows in spans
        ],
        axis=0,
    )
    w_output_all = jnp.concatenate([w_output, output_theirs], axis=0)
    branch = dot(mixed, w_output_all)
    post_attn, post_attn_plain, post_attn_inverse = norm_forward(branch, gain_post_attn)
    middle = source + post_attn
    normed2, normed2_plain, normed2_inverse = norm_forward(middle, gain_pre_ffn)
    normed2_low = normed2.astype(jnp.bfloat16)
    w_gate_all = jnp.concatenate([w_gate, gate_theirs], axis=1)
    w_up_all = jnp.concatenate([w_up, up_theirs], axis=1)
    w_down_all = jnp.concatenate([w_down, down_theirs], axis=0)
    gate_proj = dot(normed2_low, w_gate_all)
    up_proj = dot(normed2_low, w_up_all)
    activation, gelu_pull = jax.vjp(gelu_tanh, gate_proj)
    hidden = (activation * up_proj).astype(jnp.bfloat16)
    ffn_sum = dot(hidden, w_down_all)
    post_ffn, post_ffn_plain, post_ffn_inverse = norm_forward(ffn_sum, gain_post_ffn)
    layer_out = whole_rows(middle + post_ffn)

    upstream = own(out_grad).astype(jnp.float32) * valid
    grad_ffn, grad_post_ffn = norm_backward(
        upstream, post_ffn_plain, post_ffn_inverse, gain_post_ffn
    )
    grad_ffn_low = grad_ffn.astype(jnp.bfloat16)
    inner = hidden.shape[1] // 2
    down_sum = scatter_sum(
        left_dot(hidden[:, :inner], grad_ffn_low), left_dot(hidden[:, inner:], grad_ffn_low)
    )
    grad_hidden = right_dot(grad_ffn_low, w_down_all)
    grad_gate_low = gelu_pull(grad_hidden * up_proj)[0].astype(jnp.bfloat16)
    grad_up_low = (grad_hidden * activation).astype(jnp.bfloat16)
    gate_sum = scatter_sum(
        left_dot(normed2_low, grad_gate_low[:, :inner]),
        left_dot(normed2_low, grad_gate_low[:, inner:]),
    )
    up_sum = scatter_sum(
        left_dot(normed2_low, grad_up_low[:, :inner]),
        left_dot(normed2_low, grad_up_low[:, inner:]),
    )
    grad_normed2 = right_dot(grad_gate_low, w_gate_all) + right_dot(grad_up_low, w_up_all)
    grad_pre_part, grad_pre_ffn = norm_backward(
        grad_normed2, normed2_plain, normed2_inverse, gain_pre_ffn
    )
    grad_middle = upstream + grad_pre_part
    grad_branch, grad_post_attn = norm_backward(
        grad_middle, post_attn_plain, post_attn_inverse, gain_post_attn
    )
    grad_branch_low = grad_branch.astype(jnp.bfloat16)
    mixed_width = w_output.shape[0]
    output_sum = scatter_sum(
        left_dot(mixed[:, :mixed_width], grad_branch_low),
        left_dot(mixed[:, mixed_width:], grad_branch_low),
    )
    grad_mixed = right_dot(grad_branch_low, w_output_all).astype(jnp.bfloat16)

    (query_early, key_early, value_early), (query_late, key_late, value_late) = [
        attend_back(
            rows[s], lows[s], queries[s], key_states, value_states, grad_mixed[s], key_rows
        )
        for s, key_rows in spans
    ]
    grad_queries = jnp.concatenate([query_early, query_late], axis=0)
    sums = jnp.concatenate([key_late, value_late], axis=1)
    sums = jnp.concatenate(
        [sums[:half_rows] + jnp.concatenate([key_early, value_early], axis=1), sums[half_rows:]],
        axis=0,
    )
    keyvalue = own(sums) + across(others(sums))
    grad_keys, grad_values = keyvalue[:, :HD], keyvalue[:, HD:]

    query_grads, grad_gain_query = [], jnp.zeros((HD,), jnp.float32)
    for h in range(heads):
        plain, inverse = query_norms[h]
        out, gain_part = norm_backward(
            unrotate(grad_queries[:, h * HD : (h + 1) * HD], cosine_own, sine_own),
            plain,
            inverse,
            gain_query,
        )
        query_grads.append(out.astype(jnp.bfloat16))
        grad_gain_query = grad_gain_query + gain_part
    grad_query_low = jnp.concatenate(query_grads, axis=1)
    query_width = w_query.shape[1]
    query_sum = scatter_sum(
        left_dot(normed_low, grad_query_low[:, :query_width]),
        left_dot(normed_low, grad_query_low[:, query_width:]),
    )
    grad_key_pre, grad_gain_key = norm_backward(
        unrotate(grad_keys, cosine_own, sine_own), key_plain, key_inverse, gain_key
    )
    grad_key_low = grad_key_pre.astype(jnp.bfloat16)
    grad_value_low = grad_values.astype(jnp.bfloat16)
    grad_normed = (
        right_dot(grad_query_low, w_query_all)
        + right_dot(grad_key_low, w_key)
        + right_dot(grad_value_low, w_value)
    )
    grad_input_part, grad_gain_input = norm_backward(
        grad_normed, normed_plain, normed_inverse, gain_input
    )
    tokens_grad = whole_rows(grad_middle + grad_input_part)

    gains = (
        grad_gain_input,
        grad_gain_query,
        grad_gain_key,
        grad_post_attn,
        grad_pre_ffn,
        grad_post_ffn,
    )
    packed = jnp.concatenate(gains)
    size = lax.axis_size("dp")
    extra = -(-packed.shape[0] // (HD * size)) * size
    packed = jnp.pad(packed, (0, extra * HD - packed.shape[0])).reshape(extra, HD)
    with_keys = jnp.concatenate([left_dot(normed_low, grad_key_low), packed], axis=0)
    with_values = jnp.concatenate(
        [left_dot(normed_low, grad_value_low), jnp.zeros_like(packed)], axis=0
    )
    pair_sum = scatter_sum(
        jnp.where(side == 0, with_keys, with_values), jnp.where(side == 0, with_values, with_keys)
    )
    pair_other = across(pair_sum)
    pair = jnp.where(
        side == 0,
        jnp.concatenate([pair_sum, pair_other], axis=1),
        jnp.concatenate([pair_other, pair_sum], axis=1),
    )
    pair = spread(pair)
    gain_sums = pair[width:, :HD].reshape(-1)
    gain_outs, at = [], 0
    for gain in gains:
        gain_outs.append(gain_sums[at : at + gain.shape[0]])
        at += gain.shape[0]
    return (
        layer_out,
        tokens_grad,
        spread(query_sum),
        pair[:width, :HD],
        pair[:width, HD:],
        spread(output_sum),
        spread(gate_sum),
        spread(up_sum),
        spread(down_sum),
        *gain_outs,
    )


def solution(mesh):
    return jax.shard_map(
        local,
        mesh=mesh,
        in_specs=(
            P("dp", None),
            P(None, "tensor"),
            P(),
            P(),
            P("tensor", None),
            P(None, "tensor"),
            P(None, "tensor"),
            P("tensor", None),
            P(),
            P(),
            P(),
            P(),
            P(),
            P(),
            P("dp", None),
            P(),
            P(),
        ),
        out_specs=(
            P("dp", None),
            P("dp", None),
            P(None, "tensor"),
            P(),
            P(),
            P("tensor", None),
            P(None, "tensor"),
            P(None, "tensor"),
            P("tensor", None),
            P(),
            P(),
            P(),
            P(),
            P(),
            P(),
        ),
        check_vma=False,
    )
```

time: 1550 us -> 580 us (0.37)
  waiting for transfers between devices: 962 us -> 289 us
  matrix products: 203 us -> 62.4 us
  blocking collectives: 124 us -> 0 us
  starting transfers between devices: 0.99 us -> 74.9 us
  local copies, waits for them, and re-layouts: 101 us -> 34.8 us
  other arithmetic: 126 us -> 72.2 us
  Pallas kernels: 0 us -> 37.6 us
    psum x5 -> x0, waiting for transfers between devices: 507 us -> none  [the longest x1 173 us: local(): lax.psum((grad_keys_part, grad_values_part, right_dot(grad_query_low, w_q...]
    ppermute x0 -> x74, waiting for transfers between devices: none -> 289 us  [the longest x15 165 us: across(): return lax.ppermute(array, 'tensor', [(0, 1), (1, 0)])]
    reduce_scatter x5 -> x0, waiting for transfers between devices: 252 us -> none  [the longest x1 67.7 us: local(): lax.psum_scatter(grad_up, 'dp', scatter_dimension=0, tiled=True)]
    all_gather x5 -> x0, waiting for transfers between devices: 202 us -> none  [the longest x1 44.6 us: local(): lax.all_gather(all_summed[4], 'dp', axis=0, tiled=True)]
    dot_general x32 -> x7, matrix products: 156 us -> 19.7 us  [dot(): return jnp.dot(first, second, preferred_element_type=jnp.float32)]
    unnamed x2 -> x0, blocking collectives: 119 us -> none
    ppermute x0 -> x74, starting transfers between devices: none -> 74.9 us  [the longest x59 53.1 us: swap(): return lax.ppermute(array, 'dp', [(i, i ^ mask) for i in range(size)])]
    reduce_sum x9 -> x7, other arithmetic: 47.4 us -> 5.19 us  [the longest x5 4.96 us: norm_backward(): gain_grad = jnp.sum(grads_in * plain, axis=0)]
  transfers between devices with their start and end apart: 15 -> 74, of which waited for: 14 -> 37; matrix products, arithmetic and copies ran while one was open for 5% -> 19% of each run, Pallas kernels for 0% -> 3%
where the time goes in v1:
time: 580 us; the launch traced here: 575 us
  waiting for transfers between devices  289 us (50%)
  starting transfers between devices  74.9 us (13%)
  other arithmetic  72.2 us (12%)
  matrix products  62.4 us (11%)
  Pallas kernels  37.6 us (6%)
  local copies, waits for them, and re-layouts  34.8 us (6%)
    ppermute x15, waiting for transfers between devices, across(): return lax.ppermute(array, 'tensor', [(0, 1), (1, 0)])  165 us
    ppermute x59, waiting for transfers between devices, swap(): return lax.ppermute(array, 'dp', [(i, i ^ mask) for i in range(size)])  124 us
    ppermute x59, starting transfers between devices, swap(): return lax.ppermute(array, 'dp', [(i, i ^ mask) for i in range(size)])  53.1 us
    dot_general x7, matrix products, right_dot(): lax.dot_general(first, second, (((1,), (1,)), ((), ())), preferred_elemen...  26.7 us
    pallas_call x2, Pallas kernels, attend_back(): pl.pallas_call(attend_back_kernel, grid=(heads,), out_shape=(jax.ShapeDty...  23.2 us
    ppermute x15, starting transfers between devices, across(): return lax.ppermute(array, 'tensor', [(0, 1), (1, 0)])  21.8 us
    dot_general x7, matrix products, dot(): return jnp.dot(first, second, preferred_element_type=jnp.float32)  19.7 us
    dot_general x12, matrix products, left_dot(): lax.dot_general(first, second, (((0,), (0,)), ((), ())), preferred_elemen...  16.1 us
  transfers between devices with their start and end apart: 74, of which 37 were waited for; matrix products, arithmetic and copies ran while one was open for 19% of the time, Pallas kernels for 3%

profile of v1, /device:TPU:0, one launch (start us, length us, event | category | flops | bytes accessed | tf_op | source)
XLA Modules:
  0.0 574.7 jit_solution(14827985211951748341)
XLA Ops:
  3.4 2.9 collective-permute-start
  9.4 2.1 collective-permute-start.4
  11.5 2.3 convert_multiply_fusion.6
  14.0 2.2 convert_multiply_fusion.5
  20.9 2.2 constant_dynamic-slice_fusion.32
  23.1 2.2 multiply_reduce_fusion.9
  29.4 3.6 subtract_convert_fusion
  42.4 21.9 %collective-permute-done.4 = f32[320,1024]{1,0:T(8,128)} collective-permute-done((f32[320,1024]{1,0:T(8,128)}, f32[320,1024]{1,0:T(8,128)}, u32[]{:S(2)}, u32[]{:S(2)}) %collective-permute-start.4) | collective-permute-done | bytes 1310752 | tf_op jit(solution)/shard_map/ppermute | solution.py:164
  64.8 9.0 %shard_map.281 = bf16[384,1024]{1,0:T(8,128)(2,1)S(1)} custom-call(s32[384,1]{1,0:T(8,128)S(1)} %iota_add_fusion.row_ref, s32[384,1]{1,0:T(8,128)S(1)} %dynamic_slice.341.low_ref, bf16[384,1024]{1,0:T(8,128)(2,1)S(1)} %get-tuple-element.105.query_ref, bf16[1536,256]{1,0:T(8,128)(2,1)S(1)} %pad_maximum_fusion.22.key_ref, ...), custom_call_target="tpu_custom_call" | custom-call | flops 2415919104 | bytes 4194304 | tf_op jit(solution)/shard_map/pallas_call | solution.py:131
  73.9 5.3 shard_map.280
  79.2 13.2 %collective-permute-done.6 = f32[320,1024]{1,0:T(8,128)} collective-permute-done((f32[320,1024]{1,0:T(8,128)}, f32[320,1024]{1,0:T(8,128)}, u32[]{:S(2)}, u32[]{:S(2)}) %collective-permute-start.6) | collective-permute-done | bytes 1310752 | tf_op jit(solution)/shard_map/ppermute | solution.py:164
  93.9 25.7 %collective-permute-done.8 = f32[512,640]{1,0:T(8,128)} collective-permute-done((f32[512,640]{1,0:T(8,128)}, f32[512,640]{1,0:T(8,128)}, u32[]{:S(2)}, u32[]{:S(2)}) %collective-permute-start.8) | collective-permute-done | bytes 1310752 | tf_op jit(solution)/shard_map/ppermute | solution.py:164
  120.5 2.6 fusion.15
  123.1 2.3 fusion.17
  125.5 2.6 fusion.33
  128.1 6.3 %multiply_convert_fusion.1 = (bf16[768,2048]{1,0:T(8,128)(2,1)}, f32[768,2048]{1,0:T(8,128)}) fusion(f32[768,2048]{1,0:T(8,128)S(1)} %fusion.33, bf16[768,640]{1,0:T(8,128)(2,1)S(1)} %multiply_convert_fusion.4, bf16[640,1024]{1,0:T(8,128)(2,1)S(1)} %fusion.17, bf16[640,1024]{1,0:T(8,128)(2,1)S(1)} %copy-done.44), kind=kOutput, calls=%fused_computation.10 | convolution fusion | flops 2034237440 | bytes 19333120 | tf_op jit(solution)/shard_map/dot_general | solution.py:68
  134.5 2.1 fusion.19
  136.6 4.7 multiply_reduce_fusion.6
  142.2 2.0 multiply_convert_fusion.3
  144.2 13.5 %fusion.6 = (bf16[768,2048]{1,0:T(8,128)(2,1)}, bf16[768,2048]{1,0:T(8,128)(2,1)}) fusion(f32[768,2048]{1,0:T(8,128)} %copy-done.66, f32[768,2048]{1,0:T(8,128)} %get-tuple-element.133, bf16[768,640]{1,0:T(8,128)(2,1)S(1)} %get-tuple-element.84, bf16[1024,640]{1,0:T(8,128)(2,1)S(1)} %fusion.19, bf16[1024,640]{1,0:T(8,128)(2,1)S(1)} %copy-done.43), kind=kOutput, calls=%fused_computation.8 | convolution fusion | flops 2056257536 | bytes 22478848 | tf_op jit(solution)/shard_map/dot_general | solution.py:78
  157.7 4.7 fusion.30
  162.4 2.9 multiply_reduce_fusion.1
  165.3 2.1 multiply_reduce_fusion.2
  173.8 8.0 %shard_map.282 = (f32[384,1024]{1,0:T(8,128)}, f32[768,256]{1,0:T(8,128)S(1)}, f32[768,256]{1,0:T(8,128)S(1)}) custom-call(s32[384,1]{1,0:T(8,128)S(1)} %iota_add_fusion.1.row_ref, s32[384,1]{1,0:T(8,128)S(1)} %dynamic_slice.340.low_ref, bf16[384,1024]{1,0:T(8,128)(2,1)S(1)} %get-tuple-element.104.query_ref, ...), custom_call_target="tpu_custom_call" | custom-call | flops 3019898880 | bytes 8388608 | tf_op jit(solution)/shard_map/pallas_call | solution.py:150
  181.8 15.3 %shard_map.283 = (f32[384,1024]{1,0:T(8,128)S(1)}, f32[1536,256]{1,0:T(8,128)}, f32[1536,256]{1,0:T(8,128)}) custom-call(s32[384,1]{1,0:T(8,128)S(1)} %iota_add_fusion.row_ref, s32[384,1]{1,0:T(8,128)S(1)} %dynamic_slice.341.low_ref, bf16[384,1024]{1,0:T(8,128)(2,1)S(1)} %get-tuple-element.105.query_ref, bf16[1536,256]{1,0:T(8,128)(2,1)S(1)} %pad_maximum_fusion.22.key_ref, ...), custom_call_target="tpu_custom_call" | custom-call | flops 6039797760 | bytes 8388608 | tf_op jit(solution)/shard_map/pallas_call | solution.py:150
  227.2 2.9 fusion.122
  234.4 13.4 %collective-permute-done.36 = f32[256,640]{1,0:T(8,128)S(1)} collective-permute-done((f32[256,640]{1,0:T(8,128)S(1)}, f32[256,640]{1,0:T(8,128)S(1)}, u32[]{:S(2)}, u32[]{:S(2)}) %collective-permute-start.36) | collective-permute-done | bytes 655392 | tf_op jit(solution)/shard_map/ppermute | solution.py:164
  250.5 11.4 %collective-permute-done.15 = f32[320,512]{1,0:T(8,128)S(1)} collective-permute-done((f32[320,512]{1,0:T(8,128)S(1)}, f32[320,512]{1,0:T(8,128)S(1)}, u32[]{:S(2)}, u32[]{:S(2)}) %collective-permute-start.15) | collective-permute-done | bytes 655392 | tf_op jit(solution)/shard_map/ppermute | solution.py:164
  270.6 25.0 %collective-permute-done.11 = f32[768,512]{1,0:T(8,128)S(1)} collective-permute-done((f32[768,512]{1,0:T(8,128)S(1)}, f32[768,512]{1,0:T(8,128)S(1)}, u32[]{:S(2)}, u32[]{:S(2)}) %collective-permute-start.11) | collective-permute-done | bytes 1572896 | tf_op jit(solution)/shard_map/ppermute | solution.py:164
  300.6 2.3 fusion.25
  310.7 3.5 collective-permute-done.38
  316.0 3.9 collective-permute-done.17
  320.0 2.7 collective-permute-start.39
  323.1 4.6 collective-permute-done.39
  331.4 13.6 %collective-permute-done.25 = f32[328,256]{1,0:T(8,128)S(1)} collective-permute-done((f32[328,256]{1,0:T(8,128)S(1)}, f32[328,256]{1,0:T(8,128)S(1)}, u32[]{:S(2)}, u32[]{:S(2)}) %collective-permute-start.25) | collective-permute-done | bytes 335904 | tf_op jit(solution)/shard_map/ppermute | solution.py:164
  344.9 2.8 collective-permute-start.19
  355.0 2.3 collective-permute-done.41
  359.2 2.7 collective-permute-done.27
  363.7 2.7 collective-permute-start.28
  366.4 2.4 collective-permute-done.28
  376.6 24.8 %collective-permute-done.29 = f32[41,256]{1,0:T(8,128)S(1)} collective-permute-done((f32[41,256]{1,0:T(8,128)S(1)}, f32[41,256]{1,0:T(8,128)S(1)}, u32[]{:S(2)}, u32[]{:S(2)}) %collective-permute-start.29) | collective-permute-done | bytes 42016 | tf_op jit(solution)/shard_map/ppermute | solution.py:164
  403.2 4.5 maximum_select_fusion
  415.1 2.8 collective-permute-start.30
  417.9 15.3 %collective-permute-done.66 = f32[512,640]{1,0:T(8,128)} collective-permute-done((f32[512,640]{1,0:T(8,128)S(1)}, f32[512,640]{1,0:T(8,128)}, u32[]{:S(2)}, u32[]{:S(2)}) %collective-permute-start.66) | collective-permute-done | bytes 1310752 | tf_op jit(solution)/shard_map/ppermute | solution.py:164
  435.2 2.0 add_add_fusion.1
  439.3 3.5 collective-permute-done.31
  442.9 2.1 collective-permute-start.67
  447.4 3.5 collective-permute-done.47
  452.9 12.0 %collective-permute-done.57 = f32[160,1024]{1,0:T(8,128)S(1)} collective-permute-done((f32[160,1024]{1,0:T(8,128)S(1)}, f32[160,1024]{1,0:T(8,128)S(1)}, u32[]{:S(2)}, u32[]{:S(2)}) %collective-permute-start.57) | collective-permute-done | bytes 655392 | tf_op jit(solution)/shard_map/ppermute | solution.py:169
  467.0 12.0 %collective-permute-done.67 = f32[256,640]{1,0:T(8,128)S(1)} collective-permute-done((f32[256,640]{1,0:T(8,128)S(1)}, f32[256,640]{1,0:T(8,128)S(1)}, u32[]{:S(2)}, u32[]{:S(2)}) %collective-permute-start.67) | collective-permute-done | bytes 655392 | tf_op jit(solution)/shard_map/ppermute | solution.py:169
  481.1 2.6 collective-permute-start.49
  484.2 4.5 collective-permute-done.68
  488.7 3.1 collective-permute-start.69
  491.9 7.6 %collective-permute-done.49 = f32[40,1024]{1,0:T(8,128)S(1)} collective-permute-done((f32[40,1024]{1,0:T(8,128)S(1)}, f32[40,1024]{1,0:T(8,128)S(1)}, u32[]{:S(2)}, u32[]{:S(2)}) %collective-permute-start.49) | collective-permute-done | bytes 163872 | tf_op jit(solution)/shard_map/ppermute | solution.py:169
  499.6 6.9 %collective-permute-done.59 = f32[40,1024]{1,0:T(8,128)S(1)} collective-permute-done((f32[40,1024]{1,0:T(8,128)S(1)}, f32[40,1024]{1,0:T(8,128)S(1)}, u32[]{:S(2)}, u32[]{:S(2)}) %collective-permute-start.59) | collective-permute-done | bytes 163872 | tf_op jit(solution)/shard_map/ppermute | solution.py:169
  506.6 3.4 collective-permute-done.69
  510.1 6.6 %collective-permute-done.50 = f32[40,1024]{1,0:T(8,128)S(1)} collective-permute-done((f32[40,1024]{1,0:T(8,128)S(1)}, f32[40,1024]{1,0:T(8,128)S(1)}, u32[]{:S(2)}, u32[]{:S(2)}) %collective-permute-start.50) | collective-permute-done | bytes 163872 | tf_op jit(solution)/shard_map/ppermute | solution.py:169
  516.9 2.1 collective-permute-done.60
  521.4 6.4 %collective-permute-done.51 = f32[80,1024]{1,0:T(8,128)S(1)} collective-permute-done((f32[80,1024]{1,0:T(8,128)S(1)}, f32[80,1024]{1,0:T(8,128)S(1)}, u32[]{:S(2)}, u32[]{:S(2)}) %collective-permute-start.51) | collective-permute-done | bytes 327712 | tf_op jit(solution)/shard_map/ppermute | solution.py:169
  529.5 5.3 collective-permute-done.61
  539.9 2.3 maximum_select_fusion.1
  542.2 3.4 collective-permute-done.52
  545.8 13.6 %collective-permute-done.62 = f32[160,1024]{1,0:T(8,128)S(1)} collective-permute-done((f32[160,1024]{1,0:T(8,128)S(1)}, f32[160,1024]{1,0:T(8,128)S(1)}, u32[]{:S(2)}, u32[]{:S(2)}) %collective-permute-start.62) | collective-permute-done | bytes 655392 | tf_op jit(solution)/shard_map/ppermute | solution.py:169
  559.6 6.8 %collective-permute-done.72 = f32[256,640]{1,0:T(8,128)S(1)} collective-permute-done((f32[256,640]{1,0:T(8,128)S(1)}, f32[256,640]{1,0:T(8,128)S(1)}, u32[]{:S(2)}, u32[]{:S(2)}) %collective-permute-start.72) | collective-permute-done | bytes 655392 | tf_op jit(solution)/shard_map/ppermute | solution.py:169
  (461 shorter events, 155.7 us)
Async XLA Ops:
  3.4 29.8 %collective-permute-start = (f32[320,512]{1,0:T(8,128)}, f32[320,512]{1,0:T(8,128)}, u32[]{:S(2)}, u32[]{:S(2)}) collective-permute-start(f32[320,512]{1,0:T(8,128)} %convert_multiply_fusion.9), channel_id=1, source_target_pairs={{0,1},{1,0},{2,3},{3,2},{4,5},{5,4},{6,7},{7,6},{8,9},{9,8},{10,11... | collective-permute-start | bytes 1966088 | tf_op jit(solution)/shard_map/ppermute | solution.py:164
  8.2 28.1 %collective-permute-start.2 = (f32[256,640]{1,0:T(8,128)}, f32[256,640]{1,0:T(8,128)}, u32[]{:S(2)}, u32[]{:S(2)}) collective-permute-start(f32[256,640]{1,0:T(8,128)} %convert_multiply_fusion.8), channel_id=1, source_target_pairs={{0,1},{1,0},{2,3},{3,2},{4,5},{5,4},{6,7},{7,6},{8,9},{9,8},{10,11... | collective-permute-start | bytes 1966088 | tf_op jit(solution)/shard_map/ppermute | solution.py:164
  9.4 54.9 %collective-permute-start.4 = (f32[320,1024]{1,0:T(8,128)}, f32[320,1024]{1,0:T(8,128)}, u32[]{:S(2)}, u32[]{:S(2)}) collective-permute-start(f32[320,1024]{1,0:T(8,128)} %convert_multiply_fusion.7), channel_id=1, source_target_pairs={{0,1},{1,0},{2,3},{3,2},{4,5},{5,4},{6,7},{7,6},{8,9},{9,8},{10,11... | collective-permute-start | bytes 3932168 | tf_op jit(solution)/shard_map/ppermute | solution.py:164
  13.8 78.6 %collective-permute-start.6 = (f32[320,1024]{1,0:T(8,128)}, f32[320,1024]{1,0:T(8,128)}, u32[]{:S(2)}, u32[]{:S(2)}) collective-permute-start(f32[320,1024]{1,0:T(8,128)} %convert_multiply_fusion.6), channel_id=1, source_target_pairs={{0,1},{1,0},{2,3},{3,2},{4,5},{5,4},{6,7},{7,6},{8,9},{9,8},{10,11... | collective-permute-start | bytes 3932168 | tf_op jit(solution)/shard_map/ppermute | solution.py:164
  16.2 103.4 %collective-permute-start.8 = (f32[512,640]{1,0:T(8,128)}, f32[512,640]{1,0:T(8,128)}, u32[]{:S(2)}, u32[]{:S(2)}) collective-permute-start(f32[512,640]{1,0:T(8,128)} %convert_multiply_fusion.5), channel_id=1, source_target_pairs={{0,1},{1,0},{2,3},{3,2},{4,5},{5,4},{6,7},{7,6},{8,9},{9,8},{10,11... | collective-permute-start | bytes 3932168 | tf_op jit(solution)/shard_map/ppermute | solution.py:164
  64.3 56.2 %collective-permute-start.5 = (f32[320,1024]{1,0:T(8,128)}, f32[320,1024]{1,0:T(8,128)S(1)}, u32[]{:S(2)}, u32[]{:S(2)}) collective-permute-start(f32[320,1024]{1,0:T(8,128)} %collective-permute-done.4), channel_id=1, source_target_pairs={{0,2},{2,0},{4,6},{6,4},{8,10},{10,8},{12,14},{14,12},{16,18},{18,... | collective-permute-start | bytes 3932168 | tf_op jit(solution)/shard_map/ppermute | solution.py:169
  92.4 30.7 %collective-permute-start.7 = (f32[320,1024]{1,0:T(8,128)}, f32[320,1024]{1,0:T(8,128)S(1)}, u32[]{:S(2)}, u32[]{:S(2)}) collective-permute-start(f32[320,1024]{1,0:T(8,128)} %collective-permute-done.6), channel_id=1, source_target_pairs={{0,2},{2,0},{4,6},{6,4},{8,10},{10,8},{12,14},{14,12},{16,18},{18,... | collective-permute-start | bytes 3932168 | tf_op jit(solution)/shard_map/ppermute | solution.py:169
  119.7 14.8 %collective-permute-start.9 = (f32[512,640]{1,0:T(8,128)}, f32[512,640]{1,0:T(8,128)S(1)}, u32[]{:S(2)}, u32[]{:S(2)}) collective-permute-start(f32[512,640]{1,0:T(8,128)} %collective-permute-done.8), channel_id=1, source_target_pairs={{0,2},{2,0},{4,6},{6,4},{8,10},{10,8},{12,14},{14,12},{16,18},{18,... | collective-permute-start | bytes 3932168 | tf_op jit(solution)/shard_map/ppermute | solution.py:169
  210.3 19.8 %collective-permute-start.35 = (f32[256,640]{1,0:T(8,128)S(1)}, f32[256,640]{1,0:T(8,128)S(1)}, u32[]{:S(2)}, u32[]{:S(2)}) collective-permute-start(f32[256,640]{1,0:T(8,128)S(1)} %constant_dynamic-slice_fusion.17), channel_id=1, source_target_pairs={{0,2},{2,0},{4,6},{6,4},{8,10},{10,8},{12,14},{14,12},{16,18},{18,... | collective-permute-start | bytes 1966088 | tf_op jit(solution)/shard_map/ppermute | solution.py:169
  210.9 21.4 %collective-permute-start.34 = (f32[256,640]{1,0:T(8,128)S(1)}, f32[256,640]{1,0:T(8,128)S(1)}, u32[]{:S(2)}, u32[]{:S(2)}) collective-permute-start(f32[256,640]{1,0:T(8,128)S(1)} %constant_dynamic-slice_fusion.18), channel_id=1, source_target_pairs={{0,2},{2,0},{4,6},{6,4},{8,10},{10,8},{12,14},{14,12},{16,18},{18,... | collective-permute-start | bytes 1966088 | tf_op jit(solution)/shard_map/ppermute | solution.py:169
  215.8 18.2 %collective-permute-start.13 = (f32[320,512]{1,0:T(8,128)S(1)}, f32[320,512]{1,0:T(8,128)S(1)}, u32[]{:S(2)}, u32[]{:S(2)}) collective-permute-start(f32[320,512]{1,0:T(8,128)S(1)} %constant_dynamic-slice_fusion.28), channel_id=1, source_target_pairs={{0,2},{2,0},{4,6},{6,4},{8,10},{10,8},{12,14},{14,12},{16,18},{18,... | collective-permute-start | bytes 1966088 | tf_op jit(solution)/shard_map/ppermute | solution.py:169
  216.3 15.8 %collective-permute-start.14 = (f32[320,512]{1,0:T(8,128)S(1)}, f32[320,512]{1,0:T(8,128)S(1)}, u32[]{:S(2)}, u32[]{:S(2)}) collective-permute-start(f32[320,512]{1,0:T(8,128)S(1)} %constant_dynamic-slice_fusion.27), channel_id=1, source_target_pairs={{0,2},{2,0},{4,6},{6,4},{8,10},{10,8},{12,14},{14,12},{16,18},{18,... | collective-permute-start | bytes 1966088 | tf_op jit(solution)/shard_map/ppermute | solution.py:169
  217.7 47.0 %collective-permute-start.45 = (f32[320,1024]{1,0:T(8,128)S(1)}, f32[320,1024]{1,0:T(8,128)S(1)}, u32[]{:S(2)}, u32[]{:S(2)}) collective-permute-start(f32[320,1024]{1,0:T(8,128)S(1)} %constant_dynamic-slice_fusion.12), channel_id=1, source_target_pairs={{0,2},{2,0},{4,6},{6,4},{8,10},{10,8},{12,14},{14,12},{16,18},{18,... | collective-permute-start | bytes 3932168 | tf_op jit(solution)/shard_map/ppermute | solution.py:169
  230.2 17.6 %collective-permute-start.36 = (f32[256,640]{1,0:T(8,128)S(1)}, f32[256,640]{1,0:T(8,128)S(1)}, u32[]{:S(2)}, u32[]{:S(2)}) collective-permute-start(f32[256,640]{1,0:T(8,128)S(1)} %dynamic-slice_add_fusion.6), channel_id=1, source_target_pairs={{0,1},{1,0},{2,3},{3,2},{4,5},{5,4},{6,7},{7,6},{8,9},{9,8},{10,11... | collective-permute-start | bytes 1966088 | tf_op jit(solution)/shard_map/ppermute | solution.py:164
  232.1 33.9 %collective-permute-start.55 = (f32[320,1024]{1,0:T(8,128)S(1)}, f32[320,1024]{1,0:T(8,128)S(1)}, u32[]{:S(2)}, u32[]{:S(2)}) collective-permute-start(f32[320,1024]{1,0:T(8,128)S(1)} %constant_dynamic-slice_fusion.7), channel_id=1, source_target_pairs={{0,2},{2,0},{4,6},{6,4},{8,10},{10,8},{12,14},{14,12},{16,18},{18,... | collective-permute-start | bytes 3932168 | tf_op jit(solution)/shard_map/ppermute | solution.py:169
  232.3 29.6 %collective-permute-start.15 = (f32[320,512]{1,0:T(8,128)S(1)}, f32[320,512]{1,0:T(8,128)S(1)}, u32[]{:S(2)}, u32[]{:S(2)}) collective-permute-start(f32[320,512]{1,0:T(8,128)S(1)} %dynamic-slice_add_fusion.7), channel_id=1, source_target_pairs={{0,1},{1,0},{2,3},{3,2},{4,5},{5,4},{6,7},{7,6},{8,9},{9,8},{10,11... | collective-permute-start | bytes 1966088 | tf_op jit(solution)/shard_map/ppermute | solution.py:164
  234.1 34.7 %collective-permute-start.65 = (f32[512,640]{1,0:T(8,128)S(1)}, f32[512,640]{1,0:T(8,128)S(1)}, u32[]{:S(2)}, u32[]{:S(2)}) collective-permute-start(f32[512,640]{1,0:T(8,128)S(1)} %constant_dynamic-slice_fusion.2), channel_id=1, source_target_pairs={{0,2},{2,0},{4,6},{6,4},{8,10},{10,8},{12,14},{14,12},{16,18},{18,... | collective-permute-start | bytes 3932168 | tf_op jit(solution)/shard_map/ppermute | solution.py:169
  247.9 47.8 %collective-permute-start.11 = (f32[768,512]{1,0:T(8,128)S(1)}, f32[768,512]{1,0:T(8,128)S(1)}, u32[]{:S(2)}, u32[]{:S(2)}) collective-permute-start(f32[768,512]{1,0:T(8,128)S(1)} %pad_maximum_fusion.11), channel_id=1, source_target_pairs={{0,1},{1,0},{2,3},{3,2},{4,5},{5,4},{6,7},{7,6},{8,9},{9,8},{10,11... | collective-permute-start | bytes 4718600 | tf_op jit(solution)/shard_map/ppermute | solution.py:164
  261.9 107.2 %collective-permute-start.10 = (f32[768,640]{1,0:T(8,128)}, f32[768,640]{1,0:T(8,128)}, u32[]{:S(2)}, u32[]{:S(2)}) collective-permute-start(f32[768,640]{1,0:T(8,128)} %get-tuple-element.85), channel_id=1, source_target_pairs={{0,1},{1,0},{2,3},{3,2},{4,5},{5,4},{6,7},{7,6},{8,9},{9,8},{10,11... | collective-permute-start | bytes 5898248 | tf_op jit(solution)/shard_map/ppermute | solution.py:164
  264.7 104.4 %collective-permute-start.44 = (f32[320,1024]{1,0:T(8,128)}, f32[320,1024]{1,0:T(8,128)}, u32[]{:S(2)}, u32[]{:S(2)}) collective-permute-start(f32[320,1024]{1,0:T(8,128)} %constant_dynamic-slice_fusion.13), channel_id=1, source_target_pairs={{0,2},{2,0},{4,6},{6,4},{8,10},{10,8},{12,14},{14,12},{16,18},{18,... | collective-permute-start | bytes 3932168 | tf_op jit(solution)/shard_map/ppermute | solution.py:169
  266.0 39.7 %collective-permute-start.37 = (f32[128,640]{1,0:T(8,128)}, f32[128,640]{1,0:T(8,128)}, u32[]{:S(2)}, u32[]{:S(2)}) collective-permute-start(f32[128,640]{1,0:T(8,128)} %constant_dynamic-slice_fusion.16), channel_id=1, source_target_pairs={{0,4},{2,6},{4,0},{6,2},{8,12},{10,14},{12,8},{14,10},{16,20},{18,... | collective-permute-start | bytes 983048 | tf_op jit(solution)/shard_map/ppermute | solution.py:169
  268.8 38.9 %collective-permute-start.16 = (f32[160,512]{1,0:T(8,128)}, f32[160,512]{1,0:T(8,128)}, u32[]{:S(2)}, u32[]{:S(2)}) collective-permute-start(f32[160,512]{1,0:T(8,128)} %constant_dynamic-slice_fusion.26), channel_id=1, source_target_pairs={{0,4},{2,6},{4,0},{6,2},{8,12},{10,14},{12,8},{14,10},{16,20},{18,... | collective-permute-start | bytes 983048 | tf_op jit(solution)/shard_map/ppermute | solution.py:169
  304.7 18.0 %collective-permute-start.24 = (f32[328,256]{1,0:T(8,128)S(1)}, f32[328,256]{1,0:T(8,128)S(1)}, u32[]{:S(2)}, u32[]{:S(2)}) collective-permute-start(f32[328,256]{1,0:T(8,128)S(1)} %constant_dynamic-slice_fusion.22), channel_id=1, source_target_pairs={{0,2},{2,0},{4,6},{6,4},{8,10},{10,8},{12,14},{14,12},{16,18},{18,... | collective-permute-start | bytes 1007624 | tf_op jit(solution)/shard_map/ppermute | solution.py:169
  305.7 25.5 %collective-permute-start.23 = (f32[328,256]{1,0:T(8,128)S(1)}, f32[328,256]{1,0:T(8,128)S(1)}, u32[]{:S(2)}, u32[]{:S(2)}) collective-permute-start(f32[328,256]{1,0:T(8,128)S(1)} %constant_dynamic-slice_fusion.23), channel_id=1, source_target_pairs={{0,2},{2,0},{4,6},{6,4},{8,10},{10,8},{12,14},{14,12},{16,18},{18,... | collective-permute-start | bytes 1007624 | tf_op jit(solution)/shard_map/ppermute | solution.py:169
  320.0 7.7 %collective-permute-start.39 = (f32[32,640]{1,0:T(8,128)S(1)}, f32[32,640]{1,0:T(8,128)S(1)}, u32[]{:S(2)}, u32[]{:S(2)}) collective-permute-start(f32[32,640]{1,0:T(8,128)S(1)} %constant_dynamic-slice_fusion.14), channel_id=1, source_target_pairs={{0,16},{2,18},{4,20},{6,22},{8,24},{10,26},{12,28},{14,30},{16,0},... | collective-permute-start | bytes 245768 | tf_op jit(solution)/shard_map/ppermute | solution.py:169
  322.7 7.0 %collective-permute-start.18 = (f32[40,512]{1,0:T(8,128)S(1)}, f32[40,512]{1,0:T(8,128)S(1)}, u32[]{:S(2)}, u32[]{:S(2)}) collective-permute-start(f32[40,512]{1,0:T(8,128)S(1)} %constant_dynamic-slice_fusion.24), channel_id=1, source_target_pairs={{0,16},{2,18},{4,20},{6,22},{8,24},{10,26},{12,28},{14,30},{16,0},... | collective-permute-start | bytes 245768 | tf_op jit(solution)/shard_map/ppermute | solution.py:169
  327.7 17.3 %collective-permute-start.25 = (f32[328,256]{1,0:T(8,128)S(1)}, f32[328,256]{1,0:T(8,128)S(1)}, u32[]{:S(2)}, u32[]{:S(2)}) collective-permute-start(f32[328,256]{1,0:T(8,128)S(1)} %dynamic-slice_add_fusion.8), channel_id=1, source_target_pairs={{0,1},{1,0},{2,3},{3,2},{4,5},{5,4},{6,7},{7,6},{8,9},{9,8},{10,11... | collective-permute-start | bytes 1007624 | tf_op jit(solution)/shard_map/ppermute | solution.py:164
  329.7 80.6 %collective-permute-start.46 = (f32[320,1024]{1,0:T(8,128)S(1)}, f32[320,1024]{1,0:T(8,128)S(1)}, u32[]{:S(2)}, u32[]{:S(2)}) collective-permute-start(f32[320,1024]{1,0:T(8,128)S(1)} %copy-done.29), channel_id=1, source_target_pairs={{0,1},{1,0},{2,3},{3,2},{4,5},{5,4},{6,7},{7,6},{8,9},{9,8},{10,11... | collective-permute-start | bytes 3932168 | tf_op jit(solution)/shard_map/ppermute | solution.py:164
  331.3 16.6 %collective-permute-start.40 = (f32[32,640]{1,0:T(8,128)S(1)}, f32[32,640]{1,0:T(8,128)S(1)}, u32[]{:S(2)}, u32[]{:S(2)}) collective-permute-start(f32[32,640]{1,0:T(8,128)S(1)} %dynamic-slice_add_fusion.21), channel_id=1, source_target_pairs={{0,16},{2,18},{4,20},{6,22},{8,24},{10,26},{12,28},{14,30},{16,0},... | collective-permute-start | bytes 245768 | tf_op jit(solution)/shard_map/ppermute | solution.py:169
  350.3 7.0 %collective-permute-start.41 = (f32[64,640]{1,0:T(8,128)S(1)}, f32[64,640]{1,0:T(8,128)S(1)}, u32[]{:S(2)}, u32[]{:S(2)}) collective-permute-start(f32[64,640]{1,0:T(8,128)S(1)} %maximum_select_fusion.30), channel_id=1, source_target_pairs={{0,8},{2,10},{4,12},{6,14},{8,0},{10,2},{12,4},{14,6},{16,24},{18,... | collective-permute-start | bytes 491528 | tf_op jit(solution)/shard_map/ppermute | solution.py:169
  353.4 10.3 %collective-permute-start.20 = (f32[80,512]{1,0:T(8,128)S(1)}, f32[80,512]{1,0:T(8,128)S(1)}, u32[]{:S(2)}, u32[]{:S(2)}) collective-permute-start(f32[80,512]{1,0:T(8,128)S(1)} %maximum_select_fusion.29), channel_id=1, source_target_pairs={{0,8},{2,10},{4,12},{6,14},{8,0},{10,2},{12,4},{14,6},{16,24},{18,... | collective-permute-start | bytes 491528 | tf_op jit(solution)/shard_map/ppermute | solution.py:169
  361.8 10.3 %collective-permute-start.42 = (f32[128,640]{1,0:T(8,128)S(1)}, f32[128,640]{1,0:T(8,128)S(1)}, u32[]{:S(2)}, u32[]{:S(2)}) collective-permute-start(f32[128,640]{1,0:T(8,128)S(1)} %maximum_select_fusion.24), channel_id=1, source_target_pairs={{0,4},{2,6},{4,0},{6,2},{8,12},{10,14},{12,8},{14,10},{16,20},{18,... | collective-permute-start | bytes 983048 | tf_op jit(solution)/shard_map/ppermute | solution.py:169
  368.7 7.7 %collective-permute-start.21 = (f32[160,512]{1,0:T(8,128)S(1)}, f32[160,512]{1,0:T(8,128)S(1)}, u32[]{:S(2)}, u32[]{:S(2)}) collective-permute-start(f32[160,512]{1,0:T(8,128)S(1)} %maximum_select_fusion.23), channel_id=1, source_target_pairs={{0,4},{2,6},{4,0},{6,2},{8,12},{10,14},{12,8},{14,10},{16,20},{18,... | collective-permute-start | bytes 983048 | tf_op jit(solution)/shard_map/ppermute | solution.py:169
  369.0 43.6 %collective-permute-start.54 = (f32[320,1024]{1,0:T(8,128)S(1)}, f32[320,1024]{1,0:T(8,128)S(1)}, u32[]{:S(2)}, u32[]{:S(2)}) collective-permute-start(f32[320,1024]{1,0:T(8,128)S(1)} %copy-done.31), channel_id=1, source_target_pairs={{0,2},{2,0},{4,6},{6,4},{8,10},{10,8},{12,14},{14,12},{16,18},{18,... | collective-permute-start | bytes 3932168 | tf_op jit(solution)/shard_map/ppermute | solution.py:169
  369.1 43.6 %collective-permute-start.56 = (f32[320,1024]{1,0:T(8,128)S(1)}, f32[320,1024]{1,0:T(8,128)}, u32[]{:S(2)}, u32[]{:S(2)}) collective-permute-start(f32[320,1024]{1,0:T(8,128)S(1)} %copy-done.28), channel_id=1, source_target_pairs={{0,1},{1,0},{2,3},{3,2},{4,5},{5,4},{6,7},{7,6},{8,9},{9,8},{10,11... | collective-permute-start | bytes 3932168 | tf_op jit(solution)/shard_map/ppermute | solution.py:164
  372.9 28.5 %collective-permute-start.29 = (f32[41,256]{1,0:T(8,128)S(1)}, f32[41,256]{1,0:T(8,128)S(1)}, u32[]{:S(2)}, u32[]{:S(2)}) collective-permute-start(f32[41,256]{1,0:T(8,128)S(1)} %dynamic-slice_add_fusion.23), channel_id=1, source_target_pairs={{0,1},{1,0},{2,3},{3,2},{4,5},{5,4},{6,7},{7,6},{8,9},{9,8},{10,11... | collective-permute-start | bytes 125960 | tf_op jit(solution)/shard_map/ppermute | solution.py:164
  376.5 38.6 %collective-permute-start.64 = (f32[512,640]{1,0:T(8,128)S(1)}, f32[512,640]{1,0:T(8,128)}, u32[]{:S(2)}, u32[]{:S(2)}) collective-permute-start(f32[512,640]{1,0:T(8,128)S(1)} %copy-done.32), channel_id=1, source_target_pairs={{0,2},{2,0},{4,6},{6,4},{8,10},{10,8},{12,14},{14,12},{16,18},{18,... | collective-permute-start | bytes 3932168 | tf_op jit(solution)/shard_map/ppermute | solution.py:169
  401.4 31.8 %collective-permute-start.66 = (f32[512,640]{1,0:T(8,128)S(1)}, f32[512,640]{1,0:T(8,128)}, u32[]{:S(2)}, u32[]{:S(2)}) collective-permute-start(f32[512,640]{1,0:T(8,128)S(1)} %copy-done.27), channel_id=1, source_target_pairs={{0,1},{1,0},{2,3},{3,2},{4,5},{5,4},{6,7},{7,6},{8,9},{9,8},{10,11... | collective-permute-start | bytes 3932168 | tf_op jit(solution)/shard_map/ppermute | solution.py:164
  410.3 126.0 %collective-permute-start.12 = (f32[768,640]{1,0:T(8,128)S(1)}, f32[768,640]{1,0:T(8,128)S(1)}, u32[]{:S(2)}, u32[]{:S(2)}) collective-permute-start(f32[768,640]{1,0:T(8,128)S(1)} %fusion.24), channel_id=1, source_target_pairs={{0,1},{1,0},{2,3},{3,2},{4,5},{5,4},{6,7},{7,6},{8,9},{9,8},{10,11... | collective-permute-start | bytes 5898248 | tf_op jit(solution)/shard_map/ppermute | solution.py:164
  412.6 30.3 %collective-permute-start.43 = (f32[256,640]{1,0:T(8,128)S(1)}, f32[256,640]{1,0:T(8,128)S(1)}, u32[]{:S(2)}, u32[]{:S(2)}) collective-permute-start(f32[256,640]{1,0:T(8,128)S(1)} %maximum_select_fusion.18), channel_id=1, source_target_pairs={{0,2},{2,0},{4,6},{6,4},{8,10},{10,8},{12,14},{14,12},{16,18},{18,... | collective-permute-start | bytes 1966088 | tf_op jit(solution)/shard_map/ppermute | solution.py:169
  412.7 33.4 %collective-permute-start.22 = (f32[320,512]{1,0:T(8,128)S(1)}, f32[320,512]{1,0:T(8,128)S(1)}, u32[]{:S(2)}, u32[]{:S(2)}) collective-permute-start(f32[320,512]{1,0:T(8,128)S(1)} %maximum_select_fusion.17), channel_id=1, source_target_pairs={{0,2},{2,0},{4,6},{6,4},{8,10},{10,8},{12,14},{14,12},{16,18},{18,... | collective-permute-start | bytes 1966088 | tf_op jit(solution)/shard_map/ppermute | solution.py:169
  415.1 22.1 %collective-permute-start.30 = (f32[41,512]{1,0:T(8,128)S(1)}, f32[41,512]{1,0:T(8,128)S(1)}, u32[]{:S(2)}, u32[]{:S(2)}) collective-permute-start(f32[41,512]{1,0:T(8,128)S(1)} %maximum_select_fusion.31), channel_id=1, source_target_pairs={{0,16},{2,18},{4,20},{6,22},{8,24},{10,26},{12,28},{14,30},{16,0},... | collective-permute-start | bytes 251912 | tf_op jit(solution)/shard_map/ppermute | solution.py:169
  433.2 17.7 %collective-permute-start.47 = (f32[160,1024]{1,0:T(8,128)S(1)}, f32[160,1024]{1,0:T(8,128)S(1)}, u32[]{:S(2)}, u32[]{:S(2)}) collective-permute-start(f32[160,1024]{1,0:T(8,128)S(1)} %constant_dynamic-slice_fusion.11), channel_id=1, source_target_pairs={{0,4},{2,6},{4,0},{6,2},{8,12},{10,14},{12,8},{14,10},{16,20},{18,... | collective-permute-start | bytes 1966088 | tf_op jit(solution)/shard_map/ppermute | solution.py:169
  442.8 22.1 %collective-permute-start.57 = (f32[160,1024]{1,0:T(8,128)S(1)}, f32[160,1024]{1,0:T(8,128)S(1)}, u32[]{:S(2)}, u32[]{:S(2)}) collective-permute-start(f32[160,1024]{1,0:T(8,128)S(1)} %constant_dynamic-slice_fusion.6), channel_id=1, source_target_pairs={{0,4},{2,6},{4,0},{6,2},{8,12},{10,14},{12,8},{14,10},{16,20},{18,... | collective-permute-start | bytes 1966088 | tf_op jit(solution)/shard_map/ppermute | solution.py:169
  442.9 36.0 %collective-permute-start.67 = (f32[256,640]{1,0:T(8,128)S(1)}, f32[256,640]{1,0:T(8,128)S(1)}, u32[]{:S(2)}, u32[]{:S(2)}) collective-permute-start(f32[256,640]{1,0:T(8,128)S(1)} %constant_dynamic-slice_fusion.1), channel_id=1, source_target_pairs={{0,4},{2,6},{4,0},{6,2},{8,12},{10,14},{12,8},{14,10},{16,20},{18,... | collective-permute-start | bytes 1966088 | tf_op jit(solution)/shard_map/ppermute | solution.py:169
  446.1 73.0 %collective-permute-start.32 = (f32[164,512]{1,0:T(8,128)S(1)}, f32[164,512]{1,0:T(8,128)S(1)}, u32[]{:S(2)}, u32[]{:S(2)}) collective-permute-start(f32[164,512]{1,0:T(8,128)S(1)} %maximum_select_fusion.22), channel_id=1, source_target_pairs={{0,4},{2,6},{4,0},{6,2},{8,12},{10,14},{12,8},{14,10},{16,20},{18,... | collective-permute-start | bytes 1007624 | tf_op jit(solution)/shard_map/ppermute | solution.py:169
  451.0 30.0 %collective-permute-start.48 = (f32[80,1024]{1,0:T(8,128)S(1)}, f32[80,1024]{1,0:T(8,128)S(1)}, u32[]{:S(2)}, u32[]{:S(2)}) collective-permute-start(f32[80,1024]{1,0:T(8,128)S(1)} %constant_dynamic-slice_fusion.10), channel_id=1, source_target_pairs={{0,8},{2,10},{4,12},{6,14},{8,0},{10,2},{12,4},{14,6},{16,24},{18,... | collective-permute-start | bytes 983048 | tf_op jit(solution)/shard_map/ppermute | solution.py:169
  465.0 18.6 %collective-permute-start.58 = (f32[80,1024]{1,0:T(8,128)S(1)}, f32[80,1024]{1,0:T(8,128)S(1)}, u32[]{:S(2)}, u32[]{:S(2)}) collective-permute-start(f32[80,1024]{1,0:T(8,128)S(1)} %constant_dynamic-slice_fusion.5), channel_id=1, source_target_pairs={{0,8},{2,10},{4,12},{6,14},{8,0},{10,2},{12,4},{14,6},{16,24},{18,... | collective-permute-start | bytes 983048 | tf_op jit(solution)/shard_map/ppermute | solution.py:169
  479.1 9.6 %collective-permute-start.68 = (f32[128,640]{1,0:T(8,128)S(1)}, f32[128,640]{1,0:T(8,128)S(1)}, u32[]{:S(2)}, u32[]{:S(2)}) collective-permute-start(f32[128,640]{1,0:T(8,128)S(1)} %constant_dynamic-slice_fusion), channel_id=1, source_target_pairs={{0,8},{2,10},{4,12},{6,14},{8,0},{10,2},{12,4},{14,6},{16,24},{18,... | collective-permute-start | bytes 983048 | tf_op jit(solution)/shard_map/ppermute | solution.py:169
  481.1 18.4 %collective-permute-start.49 = (f32[40,1024]{1,0:T(8,128)S(1)}, f32[40,1024]{1,0:T(8,128)S(1)}, u32[]{:S(2)}, u32[]{:S(2)}) collective-permute-start(f32[40,1024]{1,0:T(8,128)S(1)} %constant_dynamic-slice_fusion.9), channel_id=1, source_target_pairs={{0,16},{2,18},{4,20},{6,22},{8,24},{10,26},{12,28},{14,30},{16,0},... | collective-permute-start | bytes 491528 | tf_op jit(solution)/shard_map/ppermute | solution.py:169
  483.7 22.8 %collective-permute-start.59 = (f32[40,1024]{1,0:T(8,128)S(1)}, f32[40,1024]{1,0:T(8,128)S(1)}, u32[]{:S(2)}, u32[]{:S(2)}) collective-permute-start(f32[40,1024]{1,0:T(8,128)S(1)} %constant_dynamic-slice_fusion.4), channel_id=1, source_target_pairs={{0,16},{2,18},{4,20},{6,22},{8,24},{10,26},{12,28},{14,30},{16,0},... | collective-permute-start | bytes 491528 | tf_op jit(solution)/shard_map/ppermute | solution.py:169
  488.7 21.3 %collective-permute-start.69 = (f32[64,640]{1,0:T(8,128)S(1)}, f32[64,640]{1,0:T(8,128)S(1)}, u32[]{:S(2)}, u32[]{:S(2)}) collective-permute-start(f32[64,640]{1,0:T(8,128)S(1)} %constant_dynamic-slice_fusion.37), channel_id=1, source_target_pairs={{0,16},{2,18},{4,20},{6,22},{8,24},{10,26},{12,28},{14,30},{16,0},... | collective-permute-start | bytes 491528 | tf_op jit(solution)/shard_map/ppermute | solution.py:169
  499.5 17.3 %collective-permute-start.50 = (f32[40,1024]{1,0:T(8,128)S(1)}, f32[40,1024]{1,0:T(8,128)S(1)}, u32[]{:S(2)}, u32[]{:S(2)}) collective-permute-start(f32[40,1024]{1,0:T(8,128)S(1)} %dynamic-slice_add_fusion.17), channel_id=1, source_target_pairs={{0,16},{2,18},{4,20},{6,22},{8,24},{10,26},{12,28},{14,30},{16,0},... | collective-permute-start | bytes 491528 | tf_op jit(solution)/shard_map/ppermute | solution.py:169
  506.5 12.5 %collective-permute-start.60 = (f32[40,1024]{1,0:T(8,128)S(1)}, f32[40,1024]{1,0:T(8,128)S(1)}, u32[]{:S(2)}, u32[]{:S(2)}) collective-permute-start(f32[40,1024]{1,0:T(8,128)S(1)} %dynamic-slice_add_fusion.16), channel_id=1, source_target_pairs={{0,16},{2,18},{4,20},{6,22},{8,24},{10,26},{12,28},{14,30},{16,0},... | collective-permute-start | bytes 491528 | tf_op jit(solution)/shard_map/ppermute | solution.py:169
  510.1 10.7 %collective-permute-start.70 = (f32[64,640]{1,0:T(8,128)S(1)}, f32[64,640]{1,0:T(8,128)S(1)}, u32[]{:S(2)}, u32[]{:S(2)}) collective-permute-start(f32[64,640]{1,0:T(8,128)S(1)} %dynamic-slice_add_fusion.15), channel_id=1, source_target_pairs={{0,16},{2,18},{4,20},{6,22},{8,24},{10,26},{12,28},{14,30},{16,0},... | collective-permute-start | bytes 491528 | tf_op jit(solution)/shard_map/ppermute | solution.py:169
  516.8 11.0 %collective-permute-start.51 = (f32[80,1024]{1,0:T(8,128)S(1)}, f32[80,1024]{1,0:T(8,128)S(1)}, u32[]{:S(2)}, u32[]{:S(2)}) collective-permute-start(f32[80,1024]{1,0:T(8,128)S(1)} %maximum_select_fusion.25), channel_id=1, source_target_pairs={{0,8},{2,10},{4,12},{6,14},{8,0},{10,2},{12,4},{14,6},{16,24},{18,... | collective-permute-start | bytes 983048 | tf_op jit(solution)/shard_map/ppermute | solution.py:169
  519.0 15.7 %collective-permute-start.61 = (f32[80,1024]{1,0:T(8,128)S(1)}, f32[80,1024]{1,0:T(8,128)S(1)}, u32[]{:S(2)}, u32[]{:S(2)}) collective-permute-start(f32[80,1024]{1,0:T(8,128)S(1)} %maximum_select_fusion.26), channel_id=1, source_target_pairs={{0,8},{2,10},{4,12},{6,14},{8,0},{10,2},{12,4},{14,6},{16,24},{18,... | collective-permute-start | bytes 983048 | tf_op jit(solution)/shard_map/ppermute | solution.py:169
  519.2 47.4 %collective-permute-start.33 = (f32[328,512]{1,0:T(8,128)S(1)}, f32[328,512]{1,0:T(8,128)S(1)}, u32[]{:S(2)}, u32[]{:S(2)}) collective-permute-start(f32[328,512]{1,0:T(8,128)S(1)} %maximum_select_fusion.16), channel_id=1, source_target_pairs={{0,2},{2,0},{4,6},{6,4},{8,10},{10,8},{12,14},{14,12},{16,18},{18,... | collective-permute-start | bytes 2015240 | tf_op jit(solution)/shard_map/ppermute | solution.py:169
  520.8 17.5 %collective-permute-start.71 = (f32[128,640]{1,0:T(8,128)S(1)}, f32[128,640]{1,0:T(8,128)S(1)}, u32[]{:S(2)}, u32[]{:S(2)}) collective-permute-start(f32[128,640]{1,0:T(8,128)S(1)} %maximum_select_fusion.27), channel_id=1, source_target_pairs={{0,8},{2,10},{4,12},{6,14},{8,0},{10,2},{12,4},{14,6},{16,24},{18,... | collective-permute-start | bytes 983048 | tf_op jit(solution)/shard_map/ppermute | solution.py:169
  527.9 17.7 %collective-permute-start.52 = (f32[160,1024]{1,0:T(8,128)S(1)}, f32[160,1024]{1,0:T(8,128)S(1)}, u32[]{:S(2)}, u32[]{:S(2)}) collective-permute-start(f32[160,1024]{1,0:T(8,128)S(1)} %maximum_select_fusion.19), channel_id=1, source_target_pairs={{0,4},{2,6},{4,0},{6,2},{8,12},{10,14},{12,8},{14,10},{16,20},{18,... | collective-permute-start | bytes 1966088 | tf_op jit(solution)/shard_map/ppermute | solution.py:169
  534.8 24.6 %collective-permute-start.62 = (f32[160,1024]{1,0:T(8,128)S(1)}, f32[160,1024]{1,0:T(8,128)S(1)}, u32[]{:S(2)}, u32[]{:S(2)}) collective-permute-start(f32[160,1024]{1,0:T(8,128)S(1)} %maximum_select_fusion.20), channel_id=1, source_target_pairs={{0,4},{2,6},{4,0},{6,2},{8,12},{10,14},{12,8},{14,10},{16,20},{18,... | collective-permute-start | bytes 1966088 | tf_op jit(solution)/shard_map/ppermute | solution.py:169
  538.3 28.2 %collective-permute-start.72 = (f32[256,640]{1,0:T(8,128)S(1)}, f32[256,640]{1,0:T(8,128)S(1)}, u32[]{:S(2)}, u32[]{:S(2)}) collective-permute-start(f32[256,640]{1,0:T(8,128)S(1)} %maximum_select_fusion.21), channel_id=1, source_target_pairs={{0,4},{2,6},{4,0},{6,2},{8,12},{10,14},{12,8},{14,10},{16,20},{18,... | collective-permute-start | bytes 1966088 | tf_op jit(solution)/shard_map/ppermute | solution.py:169
  545.8 23.4 %collective-permute-start.53 = (f32[320,1024]{1,0:T(8,128)S(1)}, f32[320,1024]{1,0:T(8,128)S(1)}, u32[]{:S(2)}, u32[]{:S(2)}) collective-permute-start(f32[320,1024]{1,0:T(8,128)S(1)} %maximum_select_fusion.13), channel_id=1, source_target_pairs={{0,2},{2,0},{4,6},{6,4},{8,10},{10,8},{12,14},{14,12},{16,18},{18,... | collective-permute-start | bytes 3932168 | tf_op jit(solution)/shard_map/ppermute | solution.py:169
  559.6 11.5 %collective-permute-start.63 = (f32[320,1024]{1,0:T(8,128)S(1)}, f32[320,1024]{1,0:T(8,128)S(1)}, u32[]{:S(2)}, u32[]{:S(2)}) collective-permute-start(f32[320,1024]{1,0:T(8,128)S(1)} %maximum_select_fusion.14), channel_id=1, source_target_pairs={{0,2},{2,0},{4,6},{6,4},{8,10},{10,8},{12,14},{14,12},{16,18},{18,... | collective-permute-start | bytes 3932168 | tf_op jit(solution)/shard_map/ppermute | solution.py:169
  (82 other events, 701.6 us)

commit v2 on v1

--- a/solution.py
+++ b/solution.py
@@ -173,11 +173,11 @@
     return (lax.axis_index("dp") // mask) % 2
 
 
-def halve(array, mask):
-    half = array.shape[0] // 2
+def halve(array, mask, axis):
+    half = array.shape[axis] // 2
     bit = bit_of(mask)
-    sent = lax.dynamic_slice_in_dim(array, (1 - bit) * half, half)
-    kept = lax.dynamic_slice_in_dim(array, bit * half, half)
+    sent = lax.dynamic_slice_in_dim(array, (1 - bit) * half, half, axis)
+    kept = lax.dynamic_slice_in_dim(array, bit * half, half, axis)
     return kept + swap(sent, mask)
 
 
@@ -190,33 +190,40 @@
     )
 
 
-def outer_masks():
+def outer_masks(first):
     size = lax.axis_size("dp")
     masks, mask = [], 2
     while mask < size:
         masks.append(mask)
         mask *= 2
-    return masks
-
-
-def scatter_sum(mine, theirs):
-    crossing = across(halve(theirs, 1))
-    total = halve(mine, 1) + crossing
-    for mask in outer_masks():
-        total = halve(total, mask)
+    return sorted(masks, key=lambda m: (m != first, m))
+
+
+def scatter_sum(array, first, axis):
+    masks = outer_masks(first)
+    array = halve(array, masks[0], axis)
+    if axis == 0:
+        inner = array.shape[1] // 2
+        mine, theirs = array[:, :inner], array[:, inner:]
+    else:
+        mine, theirs = array[0], array[1]
+    total = mine + across(theirs)
+    for mask in masks[1:]:
+        total = halve(total, mask, 0)
     return total
 
 
-def spread(total):
-    for mask in reversed(outer_masks()):
+def spread(total, first):
+    for mask in reversed(outer_masks(first)):
         total = join(total, mask)
     return join(total, 1)
 
 
-def fetch(weight, one):
-    half = weight.shape[0] // 2
-    part = lax.dynamic_slice_in_dim(weight, bit_of(1) * half, half).astype(jnp.float32)
-    theirs = join(across(part * one), 1)
+def fetch(weight, one, mask):
+    quarter = weight.shape[0] // 4
+    at = (bit_of(1) * 2 + bit_of(mask)) * quarter
+    part = lax.dynamic_slice_in_dim(weight, at, quarter).astype(jnp.float32)
+    theirs = join(join(across(part * one), mask), 1)
     return (theirs * one).astype(jnp.bfloat16)
 
 
@@ -273,11 +280,11 @@
         )
 
     one = (lengths[0] > 0).astype(jnp.float32)
-    query_theirs = fetch(w_query, one)
-    output_theirs = fetch(w_output, one)
-    gate_theirs = fetch(w_gate, one)
-    up_theirs = fetch(w_up, one)
-    down_theirs = fetch(w_down, one)
+    query_theirs = fetch(w_query, one, 2)
+    output_theirs = fetch(w_output, one, 4)
+    gate_theirs = fetch(w_gate, one, 2)
+    up_theirs = fetch(w_up, one, 4)
+    down_theirs = fetch(w_down, one, 2)
 
     used, position = layout(lengths, holder, device, tok_rows)
     cosine, sine = rotary_tables(position)
@@ -335,21 +342,12 @@
         upstream, post_ffn_plain, post_ffn_inverse, gain_post_ffn
     )
     grad_ffn_low = grad_ffn.astype(jnp.bfloat16)
-    inner = hidden.shape[1] // 2
-    down_sum = scatter_sum(
-        left_dot(hidden[:, :inner], grad_ffn_low), left_dot(hidden[:, inner:], grad_ffn_low)
-    )
+    grad_down = left_dot(hidden, grad_ffn_low).reshape(2, -1, width)
     grad_hidden = right_dot(grad_ffn_low, w_down_all)
     grad_gate_low = gelu_pull(grad_hidden * up_proj)[0].astype(jnp.bfloat16)
     grad_up_low = (grad_hidden * activation).astype(jnp.bfloat16)
-    gate_sum = scatter_sum(
-        left_dot(normed2_low, grad_gate_low[:, :inner]),
-        left_dot(normed2_low, grad_gate_low[:, inner:]),
-    )
-    up_sum = scatter_sum(
-        left_dot(normed2_low, grad_up_low[:, :inner]),
-        left_dot(normed2_low, grad_up_low[:, inner:]),
-    )
+    grad_gate = halve(left_dot(normed2_low, grad_gate_low), 1, 0)
+    grad_up = halve(left_dot(normed2_low, grad_up_low), 1, 0)
     grad_normed2 = right_dot(grad_gate_low, w_gate_all) + right_dot(grad_up_low, w_up_all)
     grad_pre_part, grad_pre_ffn = norm_backward(
         grad_normed2, normed2_plain, normed2_inverse, gain_pre_ffn
@@ -359,12 +357,15 @@
         grad_middle, post_attn_plain, post_attn_inverse, gain_post_attn
     )
     grad_branch_low = grad_branch.astype(jnp.bfloat16)
-    mixed_width = w_output.shape[0]
-    output_sum = scatter_sum(
-        left_dot(mixed[:, :mixed_width], grad_branch_low),
-        left_dot(mixed[:, mixed_width:], grad_branch_low),
-    )
+    grad_output = left_dot(mixed, grad_branch_low).reshape(2, -1, width)
+    grad_rows = jnp.concatenate([grad_down, grad_output], axis=1)
     grad_mixed = right_dot(grad_branch_low, w_output_all).astype(jnp.bfloat16)
+    grad_mixed, grad_gate, grad_up, grad_rows = lax.optimization_barrier(
+        (grad_mixed, grad_gate, grad_up, grad_rows)
+    )
+    gate_sum = scatter_sum(grad_gate, 2, 0)
+    up_sum = scatter_sum(grad_up, 4, 0)
+    rows_sum = scatter_sum(halve(grad_rows, 1, 1), 4, 1)
 
     (query_early, key_early, value_early), (query_late, key_late, value_late) = [
         attend_back(
@@ -394,10 +395,6 @@
         grad_gain_query = grad_gain_query + gain_part
     grad_query_low = jnp.concatenate(query_grads, axis=1)
     query_width = w_query.shape[1]
-    query_sum = scatter_sum(
-        left_dot(normed_low, grad_query_low[:, :query_width]),
-        left_dot(normed_low, grad_query_low[:, query_width:]),
-    )
     grad_key_pre, grad_gain_key = norm_backward(
         unrotate(grad_keys, cosine_own, sine_own), key_plain, key_inverse, gain_key
     )
@@ -425,35 +422,52 @@
     size = lax.axis_size("dp")
     extra = -(-packed.shape[0] // (HD * size)) * size
     packed = jnp.pad(packed, (0, extra * HD - packed.shape[0])).reshape(extra, HD)
-    with_keys = jnp.concatenate([left_dot(normed_low, grad_key_low), packed], axis=0)
-    with_values = jnp.concatenate(
-        [left_dot(normed_low, grad_value_low), jnp.zeros_like(packed)], axis=0
-    )
-    pair_sum = scatter_sum(
-        jnp.where(side == 0, with_keys, with_values), jnp.where(side == 0, with_values, with_keys)
-    )
+    left = side == 0
+    columns = jnp.concatenate(
+        [
+            grad_query_low[:, :query_width],
+            jnp.where(left, grad_key_low, grad_value_low),
+            grad_query_low[:, query_width:],
+            jnp.where(left, grad_value_low, grad_key_low),
+        ],
+        axis=1,
+    )
+    empty = jnp.zeros((extra, query_width), jnp.float32)
+    below = jnp.concatenate(
+        [empty, jnp.where(left, packed, 0.0), empty, jnp.where(left, 0.0, packed)], axis=1
+    )
+    grad_columns = jnp.concatenate([left_dot(normed_low, columns), below], axis=0)
+    columns_sum = scatter_sum(halve(grad_columns, 1, 0), 2, 0)
+    pair_sum = columns_sum[:, query_width:]
     pair_other = across(pair_sum)
-    pair = jnp.where(
-        side == 0,
-        jnp.concatenate([pair_sum, pair_other], axis=1),
-        jnp.concatenate([pair_other, pair_sum], axis=1),
-    )
-    pair = spread(pair)
-    gain_sums = pair[width:, :HD].reshape(-1)
+    columns_out = spread(
+        jnp.concatenate(
+            [
+                columns_sum[:, :query_width],
+                jnp.where(left, pair_sum, pair_other),
+                jnp.where(left, pair_other, pair_sum),
+            ],
+            axis=1,
+        ),
+        2,
+    )
+    gain_sums = columns_out[width:, query_width : query_width + HD].reshape(-1)
     gain_outs, at = [], 0
     for gain in gains:
         gain_outs.append(gain_sums[at : at + gain.shape[0]])
         at += gain.shape[0]
+    grad_rows_out = spread(rows_sum, 4)
+    down_rows = w_down.shape[0]
     return (
         layer_out,
         tokens_grad,
-        spread(query_sum),
-        pair[:width, :HD],
-        pair[:width, HD:],
-        spread(output_sum),
-        spread(gate_sum),
-        spread(up_sum),
-        spread(down_sum),
+        columns_out[:width, :query_width],
+        columns_out[:width, query_width : query_width + HD],
+        columns_out[:width, query_width + HD :],
+        grad_rows_out[down_rows:],
+        spread(gate_sum, 2),
+        spread(up_sum, 4),
+        grad_rows_out[:down_rows],
         *gain_outs,
     )
 

time: 580 us -> 512 us (0.88)
  waiting for transfers between devices: 289 us -> 208 us
  other arithmetic: 72.2 us -> 81.8 us
    ppermute x15 -> x13, waiting for transfers between devices: 165 us -> 115 us  [across(): return lax.ppermute(array, 'tensor', [(0, 1), (1, 0)])]
    ppermute x59 -> x42, waiting for transfers between devices: 124 us -> 93.2 us  [swap(): return lax.ppermute(array, 'dp', [(i, i ^ mask) for i in range(size)])]
    concatenate x0 -> x4, other arithmetic: none -> 9.55 us  [the longest x1 7.01 us: local(): grad_rows = jnp.concatenate([grad_down, grad_output], axis=1)]
    add x24 -> x16, other arithmetic: 6.78 us -> 15.1 us  [halve(): return kept + swap(sent, mask)]
    ppermute x15 -> x13, starting transfers between devices: 21.8 us -> 15.4 us  [across(): return lax.ppermute(array, 'tensor', [(0, 1), (1, 0)])]
    convert_element_type x5, other arithmetic: 10 us -> 3.83 us  [fetch(): return (theirs * one).astype(jnp.bfloat16)]
    select_n x24 -> x21, other arithmetic: 11.2 us -> 16.7 us  [join(): jnp.where(bit_of(mask) == 0, jnp.concatenate([array, other], axis=0), jnp...]
    ppermute x59 -> x42, starting transfers between devices: 53.1 us -> 56.3 us  [swap(): return lax.ppermute(array, 'dp', [(i, i ^ mask) for i in range(size)])]
  transfers between devices with their start and end apart: 74 -> 55, of which waited for: 37 -> 22; matrix products, arithmetic and copies ran while one was open for 19% -> 26% of each run, Pallas kernels for 3% -> 7%
where the time goes in v2:
time: 512 us; the launch traced here: 505 us
  waiting for transfers between devices  208 us (41%)
  other arithmetic  81.8 us (16%)
  starting transfers between devices  71.6 us (14%)
  matrix products  64.5 us (13%)
  Pallas kernels  37.7 us (7%)
  local copies, waits for them, and re-layouts  37.2 us (7%)
    ppermute x13, waiting for transfers between devices, across(): return lax.ppermute(array, 'tensor', [(0, 1), (1, 0)])  115 us
    ppermute x42, waiting for transfers between devices, swap(): return lax.ppermute(array, 'dp', [(i, i ^ mask) for i in range(size)])  93.2 us
    ppermute x42, starting transfers between devices, swap(): return lax.ppermute(array, 'dp', [(i, i ^ mask) for i in range(size)])  56.3 us
    dot_general x7, matrix products, right_dot(): lax.dot_general(first, second, (((1,), (1,)), ((), ())), preferred_elemen...  30.4 us
    pallas_call x2, Pallas kernels, attend_back(): pl.pallas_call(attend_back_kernel, grid=(heads,), out_shape=(jax.ShapeDty...  23.3 us
    dot_general x7, matrix products, dot(): return jnp.dot(first, second, preferred_element_type=jnp.float32)  17.4 us
    select_n x21, other arithmetic, join(): jnp.where(bit_of(mask) == 0, jnp.concatenate([array, other], axis=0), jnp...  16.7 us
    dot_general x5, matrix products, left_dot(): lax.dot_general(first, second, (((0,), (0,)), ((), ())), preferred_elemen...  16.7 us
  transfers between devices with their start and end apart: 55, of which 22 were waited for; matrix products, arithmetic and copies ran while one was open for 26% of the time, Pallas kernels for 7%

profile of v2, /device:TPU:0, one launch (start us, length us, event | category | flops | bytes accessed | tf_op | source)
XLA Modules:
  0.0 505.3 jit_solution(4614461502568922229)
XLA Ops:
  3.3 2.9 collective-permute-start
  9.8 2.0 collective-permute-start.12
  15.5 2.0 collective-permute-start.6
  21.3 2.2 multiply_reduce_fusion.9
  26.4 3.6 subtract_convert_fusion
  32.8 30.6 %collective-permute-done.6 = f32[160,1024]{1,0:T(8,128)} collective-permute-done((f32[160,1024]{1,0:T(8,128)}, f32[160,1024]{1,0:T(8,128)}, u32[]{:S(2)}, u32[]{:S(2)}) %collective-permute-start.6) | collective-permute-done | bytes 655392 | tf_op jit(solution)/shard_map/ppermute | solution.py:164
  69.6 18.2 %collective-permute-done.4 = f32[128,640]{1,0:T(8,128)S(1)} collective-permute-done((f32[128,640]{1,0:T(8,128)}, f32[128,640]{1,0:T(8,128)S(1)}, u32[]{:S(2)}, u32[]{:S(2)}) %collective-permute-start.4) | collective-permute-done | bytes 327712 | tf_op jit(solution)/shard_map/ppermute | solution.py:169
  91.5 2.0 maximum_select_fusion.14
  99.4 9.0 %shard_map.281 = bf16[384,1024]{1,0:T(8,128)(2,1)S(1)} custom-call(s32[384,1]{1,0:T(8,128)S(1)} %iota_add_fusion.row_ref, s32[384,1]{1,0:T(8,128)S(1)} %dynamic_slice.229.low_ref, bf16[384,1024]{1,0:T(8,128)(2,1)S(1)} %get-tuple-element.124.query_ref, bf16[1536,256]{1,0:T(8,128)(2,1)S(1)} %pad_maximum_fusion.24.key_ref, ...), custom_call_target="tpu_custom_call" | custom-call | flops 2415919104 | bytes 4194304 | tf_op jit(solution)/shard_map/pallas_call | solution.py:131
  108.6 5.3 %shard_map.280 = bf16[384,1024]{1,0:T(8,128)(2,1)S(1)} custom-call(s32[384,1]{1,0:T(8,128)S(1)} %iota_add_fusion.1.row_ref, s32[384,1]{1,0:T(8,128)S(1)} %dynamic_slice.228.low_ref, bf16[384,1024]{1,0:T(8,128)(2,1)S(1)} %get-tuple-element.123.query_ref, bf16[1536,256]{1,0:T(8,128)(2,1)S(1)} %pad_maximum_fusion.24.key_ref, ...), custom_call_target="tpu_custom_call" | custom-call | flops 1207959552 | bytes 4194304 | tf_op jit(solution)/shard_map/pallas_call | solution.py:131
  116.8 2.7 fusion.17
  119.6 2.6 fusion.33
  122.2 6.0 %multiply_convert_fusion.1 = (bf16[768,2048]{1,0:T(8,128)(2,1)S(1)}, f32[768,2048]{1,0:T(8,128)}) fusion(f32[768,2048]{1,0:T(8,128)S(1)} %fusion.33, bf16[768,640]{1,0:T(8,128)(2,1)S(1)} %multiply_convert_fusion.4, bf16[640,1024]{1,0:T(8,128)(2,1)S(1)} %fusion.17, bf16[640,1024]{1,0:T(8,128)(2,1)S(1)} %copy-done.46), kind=kOutput, calls=%fused_computation.11 | convolution fusion | flops 2034237440 | bytes 19333120 | tf_op jit(solution)/shard_map/dot_general | solution.py:68
  130.5 2.7 multiply_reduce_fusion.6
  133.3 2.1 multiply_reduce_fusion
  135.5 12.7 %fusion.6 = (bf16[768,2048]{1,0:T(8,128)(2,1)}, bf16[768,2048]{1,0:T(8,128)(2,1)}) fusion(f32[768,2048]{1,0:T(8,128)} %copy-done.61, f32[768,2048]{1,0:T(8,128)} %get-tuple-element.152, bf16[1024,640]{1,0:T(8,128)(2,1)} %copy-done.37, bf16[1024,640]{1,0:T(8,128)(2,1)} %param.24, f32[768,640]{1,0:T(8,128)S(1)} %get-tuple-element.154, ...), kind=kOutput, calls=%fused_computation.9 | convolution fusion | flops 2061664256 | bytes 24456704 | tf_op jit(solution)/shard_map/dot_general | solution.py:78
  148.2 6.3 %fusion.30 = f32[768,640]{1,0:T(8,128)} fusion(bf16[768,2048]{1,0:T(8,128)(2,1)} %get-tuple-element.77, bf16[640,1024]{1,0:T(8,128)(2,1)S(1)} %copy-done.36, bf16[640,1024]{1,0:T(8,128)(2,1)} %param.23), kind=kOutput, calls=%fused_computation.86 | convolution fusion | flops 2018508800 | bytes 7733248 | tf_op jit(solution)/shard_map/dot_general | solution.py:78
  154.6 2.3 fusion.101
  156.9 2.3 fusion.100
  160.5 6.0 %multiply_reduce_fusion.1 = (f32[640]{0:T(1024)S(1)}, f32[768]{0:T(1024)S(1)}, f32[768,640]{1,0:T(8,128)S(1)}) fusion(f32[768,640]{1,0:T(8,128)S(1)} %get-tuple-element.73, f32[768]{0:T(1024)S(1)} %add_rsqrt_fusion.4, f32[640]{0:T(1024)S(1)} %broadcast_add_fusion.1, f32[768,640]{1,0:T(8,128)} %fusion.30, bf16[768,2048]{1,0:T(8,128)(2,1)S(1)} %copy-done.25, ...), kind=kOutput, calls=%fused_computation.67 | convolution fusion | flops 2021948032 | bytes 11676672 | tf_op jit(solution)/shard_map/dot_general | solution.py:78
  171.9 2.2 multiply_reduce_fusion.2
  176.2 2.6 convolution_convert_fusion.1
  178.7 3.0 fusion.93
  181.7 3.0 fusion.47
  184.6 5.4 %fusion.87 = f32[2048,640]{1,0:T(8,128)} fusion(bf16[768,2048]{1,0:T(8,128)(2,1)S(1)} %copy-done.63, f32[768,640]{1,0:T(8,128)S(1)} %copy-done.28, f32[768]{0:T(1024)S(1)} %broadcast_multiply_fusion.8, f32[768]{0:T(1024)S(1)} %maximum_reduce_fusion, f32[640]{0:T(1024)S(1)} %broadcast_add_fusion, f32[768]{0:T(1024)S(1)} %add_rsqrt_fusion.3, ...), kind=kOutput, calls=%fused_computation.332 | convolution fusion | flops 2018672640 | bytes 11349504 | tf_op jit(solution)/shard_map/dot_general | solution.py:72
  190.0 7.0 %pad_maximum_fusion = f32[2,1536,640]{2,1,0:T(8,128)} fusion(f32[2,512,640]{2,1,0:T(8,128)} %bitcast.38, f32[2,1024,640]{2,1,0:T(8,128)} %bitcast.37), kind=kLoop, calls=%fused_computation.2 | loop fusion | flops 1966080 | bytes 15728640 | tf_op jit(solution)/shard_map/concatenate | solution.py:361
  197.1 4.5 dynamic-slice_add_fusion.2
  201.6 3.7 dynamic-slice_add_fusion.1
  205.4 8.0 %shard_map.282 = (f32[384,1024]{1,0:T(8,128)}, f32[768,256]{1,0:T(8,128)S(1)}, f32[768,256]{1,0:T(8,128)S(1)}) custom-call(s32[384,1]{1,0:T(8,128)S(1)} %iota_add_fusion.1.row_ref, s32[384,1]{1,0:T(8,128)S(1)} %dynamic_slice.228.low_ref, bf16[384,1024]{1,0:T(8,128)(2,1)S(1)} %get-tuple-element.123.query_ref, ...), custom_call_target="tpu_custom_call" | custom-call | flops 3019898880 | bytes 8388608 | tf_op jit(solution)/shard_map/pallas_call | solution.py:150
  213.4 15.3 %shard_map.283 = (f32[384,1024]{1,0:T(8,128)S(1)}, f32[1536,256]{1,0:T(8,128)}, f32[1536,256]{1,0:T(8,128)}) custom-call(s32[384,1]{1,0:T(8,128)S(1)} %iota_add_fusion.row_ref, s32[384,1]{1,0:T(8,128)S(1)} %dynamic_slice.229.low_ref, bf16[384,1024]{1,0:T(8,128)(2,1)S(1)} %get-tuple-element.124.query_ref, bf16[1536,256]{1,0:T(8,128)(2,1)S(1)} %pad_maximum_fusion.24.key_ref, ...), custom_call_target="tpu_custom_call" | custom-call | flops 6039797760 | bytes 8388608 | tf_op jit(solution)/shard_map/pallas_call | solution.py:150
  240.0 2.2 constant_dynamic-slice_fusion.7
  244.4 30.2 %collective-permute-done.18 = f32[768,512]{1,0:T(8,128)S(1)} collective-permute-done((f32[768,512]{1,0:T(8,128)S(1)}, f32[768,512]{1,0:T(8,128)S(1)}, u32[]{:S(2)}, u32[]{:S(2)}) %collective-permute-start.18) | collective-permute-done | bytes 1572896 | tf_op jit(solution)/shard_map/ppermute | solution.py:164
  281.0 3.7 fusion.62
  284.8 2.4 maximum_maximum_fusion
  295.7 2.6 dynamic-slice_add_fusion
  300.4 8.2 %collective-permute-done.48 = f32[160,1024]{1,0:T(8,128)} collective-permute-done((f32[160,1024]{1,0:T(8,128)S(1)}, f32[160,1024]{1,0:T(8,128)}, u32[]{:S(2)}, u32[]{:S(2)}) %collective-permute-start.48) | collective-permute-done | bytes 655392 | tf_op jit(solution)/shard_map/ppermute | solution.py:164
  311.0 11.5 %collective-permute-done.40 = f32[160,1024]{1,0:T(8,128)S(1)} collective-permute-done((f32[160,1024]{1,0:T(8,128)S(1)}, f32[160,1024]{1,0:T(8,128)S(1)}, u32[]{:S(2)}, u32[]{:S(2)}) %collective-permute-start.40) | collective-permute-done | bytes 655392 | tf_op jit(solution)/shard_map/ppermute | solution.py:164
  323.8 12.5 %collective-permute-done.49 = f32[80,1024]{1,0:T(8,128)S(1)} collective-permute-done((f32[80,1024]{1,0:T(8,128)S(1)}, f32[80,1024]{1,0:T(8,128)S(1)}, u32[]{:S(2)}, u32[]{:S(2)}) %collective-permute-start.49) | collective-permute-done | bytes 327712 | tf_op jit(solution)/shard_map/ppermute | solution.py:169
  338.0 2.7 collective-permute-start.50
  340.9 6.9 %collective-permute-done.31 = f32[2,384,640]{2,1,0:T(8,128)S(1)} collective-permute-done((f32[2,384,640]{2,1,0:T(8,128)S(1)}, f32[2,384,640]{2,1,0:T(8,128)S(1)}, u32[]{:S(2)}, u32[]{:S(2)}) %collective-permute-start.31) | collective-permute-done | bytes 1966112 | tf_op jit(solution)/shard_map/ppermute | solution.py:169
  349.4 2.6 collective-permute-done.41
  353.7 22.0 %collective-permute-done.22 = f32[164,768]{1,0:T(8,128)S(1)} collective-permute-done((f32[164,768]{1,0:T(8,128)S(1)}, f32[164,768]{1,0:T(8,128)S(1)}, u32[]{:S(2)}, u32[]{:S(2)}) %collective-permute-start.22) | collective-permute-done | bytes 503840 | tf_op jit(solution)/shard_map/ppermute | solution.py:164
  377.2 2.7 collective-permute-start.42
  379.9 4.8 collective-permute-done.23
  385.6 9.1 %collective-permute-done.32 = f32[384,640]{1,0:T(8,128)S(1)} collective-permute-done((f32[384,640]{1,0:T(8,128)S(1)}, f32[384,640]{1,0:T(8,128)S(1)}, u32[]{:S(2)}, u32[]{:S(2)}) %collective-permute-start.32) | collective-permute-done | bytes 983072 | tf_op jit(solution)/shard_map/ppermute | solution.py:164
  396.2 2.7 collective-permute-start.24
  398.9 5.1 %collective-permute-done.24 = f32[41,768]{1,0:T(8,128)S(1)} collective-permute-done((f32[41,768]{1,0:T(8,128)S(1)}, f32[41,768]{1,0:T(8,128)S(1)}, u32[]{:S(2)}, u32[]{:S(2)}) %collective-permute-start.24) | collective-permute-done | bytes 125984 | tf_op jit(solution)/shard_map/ppermute | solution.py:169
  406.8 3.5 collective-permute-done.25
  410.2 2.6 collective-permute-start.34
  412.9 7.0 %collective-permute-done.34 = f32[96,640]{1,0:T(8,128)S(1)} collective-permute-done((f32[96,640]{1,0:T(8,128)S(1)}, f32[96,640]{1,0:T(8,128)S(1)}, u32[]{:S(2)}, u32[]{:S(2)}) %collective-permute-start.34) | collective-permute-done | bytes 245792 | tf_op jit(solution)/shard_map/ppermute | solution.py:169
  420.1 2.8 collective-permute-start.35
  422.9 4.4 collective-permute-start.52
  427.4 5.4 %collective-permute-done.26 = f32[41,1024]{1,0:T(8,128)S(1)} collective-permute-done((f32[41,1024]{1,0:T(8,128)S(1)}, f32[41,1024]{1,0:T(8,128)S(1)}, u32[]{:S(2)}, u32[]{:S(2)}) %collective-permute-start.26) | collective-permute-done | bytes 167968 | tf_op jit(solution)/shard_map/ppermute | solution.py:169
  432.8 10.4 %collective-permute-start.44 = (f32[80,1024]{1,0:T(8,128)S(1)}, f32[80,1024]{1,0:T(8,128)S(1)}, u32[]{:S(2)}, u32[]{:S(2)}) collective-permute-start(f32[80,1024]{1,0:T(8,128)S(1)} %maximum_select_fusion.26), channel_id=1, source_target_pairs={{0,8},{2,10},{4,12},{6,14},{8,0},{10,2},{12,4},{14,6},{16,24},{18,... | collective-permute-start | bytes 983048 | tf_op jit(solution)/shard_map/ppermute | solution.py:169
  443.2 5.2 %collective-permute-start.27 = (f32[82,1024]{1,0:T(8,128)S(1)}, f32[82,1024]{1,0:T(8,128)S(1)}, u32[]{:S(2)}, u32[]{:S(2)}) collective-permute-start(f32[82,1024]{1,0:T(8,128)S(1)} %maximum_select_fusion.25), channel_id=1, source_target_pairs={{0,8},{2,10},{4,12},{6,14},{8,0},{10,2},{12,4},{14,6},{16,24},{18,... | collective-permute-start | bytes 1007624 | tf_op jit(solution)/shard_map/ppermute | solution.py:169
  452.8 6.7 %collective-permute-done.27 = f32[82,1024]{1,0:T(8,128)S(1)} collective-permute-done((f32[82,1024]{1,0:T(8,128)S(1)}, f32[82,1024]{1,0:T(8,128)S(1)}, u32[]{:S(2)}, u32[]{:S(2)}) %collective-permute-start.27) | collective-permute-done | bytes 335904 | tf_op jit(solution)/shard_map/ppermute | solution.py:169
  459.7 3.0 collective-permute-done.36
  462.9 4.5 maximum_select_fusion
  467.4 6.2 %collective-permute-done.53 = f32[160,1024]{1,0:T(8,128)S(1)} collective-permute-done((f32[160,1024]{1,0:T(8,128)S(1)}, f32[160,1024]{1,0:T(8,128)S(1)}, u32[]{:S(2)}, u32[]{:S(2)}) %collective-permute-start.53) | collective-permute-done | bytes 655392 | tf_op jit(solution)/shard_map/ppermute | solution.py:169
  474.6 5.3 %collective-permute-done.28 = f32[164,1024]{1,0:T(8,128)S(1)} collective-permute-done((f32[164,1024]{1,0:T(8,128)S(1)}, f32[164,1024]{1,0:T(8,128)S(1)}, u32[]{:S(2)}, u32[]{:S(2)}) %collective-permute-start.28) | collective-permute-done | bytes 671776 | tf_op jit(solution)/shard_map/ppermute | solution.py:169
  480.3 7.4 %collective-permute-done.37 = f32[384,640]{1,0:T(8,128)S(1)} collective-permute-done((f32[384,640]{1,0:T(8,128)S(1)}, f32[384,640]{1,0:T(8,128)S(1)}, u32[]{:S(2)}, u32[]{:S(2)}) %collective-permute-start.37) | collective-permute-done | bytes 983072 | tf_op jit(solution)/shard_map/ppermute | solution.py:169
  488.1 2.3 maximum_select_fusion.1
  490.4 3.7 maximum_select_fusion.8
  494.1 3.8 maximum_select_fusion.7
  (403 shorter events, 106.8 us)
Async XLA Ops:
  0.6 20.7 %copy-start = (bf16[640,256]{1,0:T(8,128)(2,1)S(1)}, bf16[640,256]{1,0:T(8,128)(2,1)}, u32[]{:S(2)}) copy-start(bf16[640,256]{1,0:T(8,128)(2,1)} %param.19) | copy-start | bytes 983044
  1.4 16.2 %copy-start.59 = (s32[24]{0:T(128)S(1)}, s32[24]{0:T(128)}, u32[]{:S(2)}) copy-start(s32[24]{0:T(128)} %param.32) | copy-start | bytes 292
  1.4 16.5 %copy-start.57 = (f32[256]{0:T(256)S(1)}, f32[256]{0:T(256)}, u32[]{:S(2)}) copy-start(f32[256]{0:T(256)} %param.27) | copy-start | bytes 3076
  1.4 16.5 %copy-start.53 = (f32[640]{0:T(1024)S(1)}, f32[640]{0:T(1024)}, u32[]{:S(2)}) copy-start(f32[640]{0:T(1024)} %param.25) | copy-start | bytes 7684
  1.4 16.5 %copy-start.54 = (f32[640]{0:T(1024)S(1)}, f32[640]{0:T(1024)}, u32[]{:S(2)}) copy-start(f32[640]{0:T(1024)} %param.28) | copy-start | bytes 7684
  1.4 16.5 %copy-start.55 = (f32[640]{0:T(1024)S(1)}, f32[640]{0:T(1024)}, u32[]{:S(2)}) copy-start(f32[640]{0:T(1024)} %param.29) | copy-start | bytes 7684
  1.5 16.5 %copy-start.56 = (f32[640]{0:T(1024)S(1)}, f32[640]{0:T(1024)}, u32[]{:S(2)}) copy-start(f32[640]{0:T(1024)} %param.30) | copy-start | bytes 7684
  1.5 16.5 %copy-start.19 = (bf16[1536,640]{1,0:T(8,128)(2,1)S(1)}, bf16[1536,640]{1,0:T(8,128)(2,1)}, u32[]{:S(2)}) copy-start(bf16[1536,640]{1,0:T(8,128)(2,1)} %param.17) | copy-start | bytes 5898244
  3.3 27.9 %collective-permute-start = (f32[160,512]{1,0:T(8,128)}, f32[160,512]{1,0:T(8,128)}, u32[]{:S(2)}, u32[]{:S(2)}) collective-permute-start(f32[160,512]{1,0:T(8,128)} %convert_multiply_fusion.9), channel_id=1, source_target_pairs={{0,1},{1,0},{2,3},{3,2},{4,5},{5,4},{6,7},{7,6},{8,9},{9,8},{10,11... | collective-permute-start | bytes 983048 | tf_op jit(solution)/shard_map/ppermute | solution.py:164
  7.9 59.6 %collective-permute-start.3 = (f32[128,640]{1,0:T(8,128)}, f32[128,640]{1,0:T(8,128)}, u32[]{:S(2)}, u32[]{:S(2)}) collective-permute-start(f32[128,640]{1,0:T(8,128)} %convert_multiply_fusion.8), channel_id=1, source_target_pairs={{0,1},{1,0},{2,3},{3,2},{4,5},{5,4},{6,7},{7,6},{8,9},{9,8},{10,11... | collective-permute-start | bytes 983048 | tf_op jit(solution)/shard_map/ppermute | solution.py:164
  9.8 58.3 %collective-permute-start.12 = (f32[256,640]{1,0:T(8,128)}, f32[256,640]{1,0:T(8,128)}, u32[]{:S(2)}, u32[]{:S(2)}) collective-permute-start(f32[256,640]{1,0:T(8,128)} %convert_multiply_fusion.5), channel_id=1, source_target_pairs={{0,1},{1,0},{2,3},{3,2},{4,5},{5,4},{6,7},{7,6},{8,9},{9,8},{10,11... | collective-permute-start | bytes 1966088 | tf_op jit(solution)/shard_map/ppermute | solution.py:164
  13.7 51.6 %collective-permute-start.9 = (f32[160,1024]{1,0:T(8,128)}, f32[160,1024]{1,0:T(8,128)}, u32[]{:S(2)}, u32[]{:S(2)}) collective-permute-start(f32[160,1024]{1,0:T(8,128)} %convert_multiply_fusion.6), channel_id=1, source_target_pairs={{0,1},{1,0},{2,3},{3,2},{4,5},{5,4},{6,7},{7,6},{8,9},{9,8},{10,11... | collective-permute-start | bytes 1966088 | tf_op jit(solution)/shard_map/ppermute | solution.py:164
  15.5 47.9 %collective-permute-start.6 = (f32[160,1024]{1,0:T(8,128)}, f32[160,1024]{1,0:T(8,128)}, u32[]{:S(2)}, u32[]{:S(2)}) collective-permute-start(f32[160,1024]{1,0:T(8,128)} %convert_multiply_fusion.7), channel_id=1, source_target_pairs={{0,1},{1,0},{2,3},{3,2},{4,5},{5,4},{6,7},{7,6},{8,9},{9,8},{10,11... | collective-permute-start | bytes 1966088 | tf_op jit(solution)/shard_map/ppermute | solution.py:164
  31.2 37.2 %collective-permute-start.1 = (f32[160,512]{1,0:T(8,128)}, f32[160,512]{1,0:T(8,128)S(1)}, u32[]{:S(2)}, u32[]{:S(2)}) collective-permute-start(f32[160,512]{1,0:T(8,128)} %collective-permute-done), channel_id=1, source_target_pairs={{0,4},{2,6},{4,0},{6,2},{8,12},{10,14},{12,8},{14,10},{16,20},{18,... | collective-permute-start | bytes 983048 | tf_op jit(solution)/shard_map/ppermute | solution.py:169
  63.4 25.6 %collective-permute-start.7 = (f32[160,1024]{1,0:T(8,128)}, f32[160,1024]{1,0:T(8,128)}, u32[]{:S(2)}, u32[]{:S(2)}) collective-permute-start(f32[160,1024]{1,0:T(8,128)} %collective-permute-done.6), channel_id=1, source_target_pairs={{0,4},{2,6},{4,0},{6,2},{8,12},{10,14},{12,8},{14,10},{16,20},{18,... | collective-permute-start | bytes 1966088 | tf_op jit(solution)/shard_map/ppermute | solution.py:169
  65.3 26.2 %collective-permute-start.10 = (f32[160,1024]{1,0:T(8,128)}, f32[160,1024]{1,0:T(8,128)}, u32[]{:S(2)}, u32[]{:S(2)}) collective-permute-start(f32[160,1024]{1,0:T(8,128)} %collective-permute-done.9), channel_id=1, source_target_pairs={{0,8},{2,10},{4,12},{6,14},{8,0},{10,2},{12,4},{14,6},{16,24},{18,... | collective-permute-start | bytes 1966088 | tf_op jit(solution)/shard_map/ppermute | solution.py:169
  67.5 20.3 %collective-permute-start.4 = (f32[128,640]{1,0:T(8,128)}, f32[128,640]{1,0:T(8,128)S(1)}, u32[]{:S(2)}, u32[]{:S(2)}) collective-permute-start(f32[128,640]{1,0:T(8,128)} %collective-permute-done.3), channel_id=1, source_target_pairs={{0,8},{2,10},{4,12},{6,14},{8,0},{10,2},{12,4},{14,6},{16,24},{18,... | collective-permute-start | bytes 983048 | tf_op jit(solution)/shard_map/ppermute | solution.py:169
  68.1 25.5 %collective-permute-start.13 = (f32[256,640]{1,0:T(8,128)}, f32[256,640]{1,0:T(8,128)S(1)}, u32[]{:S(2)}, u32[]{:S(2)}) collective-permute-start(f32[256,640]{1,0:T(8,128)} %collective-permute-done.12), channel_id=1, source_target_pairs={{0,4},{2,6},{4,0},{6,2},{8,12},{10,14},{12,8},{14,10},{16,20},{18,... | collective-permute-start | bytes 1966088 | tf_op jit(solution)/shard_map/ppermute | solution.py:169
  69.5 26.0 %collective-permute-start.2 = (f32[320,512]{1,0:T(8,128)S(1)}, f32[320,512]{1,0:T(8,128)S(1)}, u32[]{:S(2)}, u32[]{:S(2)}) collective-permute-start(f32[320,512]{1,0:T(8,128)S(1)} %maximum_select_fusion.20), channel_id=1, source_target_pairs={{0,2},{2,0},{4,6},{6,4},{8,10},{10,8},{12,14},{14,12},{16,18},{18,... | collective-permute-start | bytes 1966088 | tf_op jit(solution)/shard_map/ppermute | solution.py:169
  89.0 19.4 %collective-permute-start.5 = (f32[256,640]{1,0:T(8,128)S(1)}, f32[256,640]{1,0:T(8,128)S(1)}, u32[]{:S(2)}, u32[]{:S(2)}) collective-permute-start(f32[256,640]{1,0:T(8,128)S(1)} %maximum_select_fusion.21), channel_id=1, source_target_pairs={{0,2},{2,0},{4,6},{6,4},{8,10},{10,8},{12,14},{14,12},{16,18},{18,... | collective-permute-start | bytes 1966088 | tf_op jit(solution)/shard_map/ppermute | solution.py:169
  90.9 25.4 %collective-permute-start.8 = (f32[320,1024]{1,0:T(8,128)S(1)}, f32[320,1024]{1,0:T(8,128)S(1)}, u32[]{:S(2)}, u32[]{:S(2)}) collective-permute-start(f32[320,1024]{1,0:T(8,128)S(1)} %maximum_select_fusion.13), channel_id=1, source_target_pairs={{0,2},{2,0},{4,6},{6,4},{8,10},{10,8},{12,14},{14,12},{16,18},{18,... | collective-permute-start | bytes 3932168 | tf_op jit(solution)/shard_map/ppermute | solution.py:169
  93.5 23.3 %collective-permute-start.11 = (f32[320,1024]{1,0:T(8,128)S(1)}, f32[320,1024]{1,0:T(8,128)}, u32[]{:S(2)}, u32[]{:S(2)}) collective-permute-start(f32[320,1024]{1,0:T(8,128)S(1)} %maximum_select_fusion.14), channel_id=1, source_target_pairs={{0,2},{2,0},{4,6},{6,4},{8,10},{10,8},{12,14},{14,12},{16,18},{18,... | collective-permute-start | bytes 3932168 | tf_op jit(solution)/shard_map/ppermute | solution.py:169
  95.1 33.2 %collective-permute-start.14 = (f32[512,640]{1,0:T(8,128)S(1)}, f32[512,640]{1,0:T(8,128)S(1)}, u32[]{:S(2)}, u32[]{:S(2)}) collective-permute-start(f32[512,640]{1,0:T(8,128)S(1)} %maximum_select_fusion.15), channel_id=1, source_target_pairs={{0,2},{2,0},{4,6},{6,4},{8,10},{10,8},{12,14},{14,12},{16,18},{18,... | collective-permute-start | bytes 3932168 | tf_op jit(solution)/shard_map/ppermute | solution.py:169
  166.5 282.0 %collective-permute-start.15 = (f32[768,640]{1,0:T(8,128)}, f32[768,640]{1,0:T(8,128)}, u32[]{:S(2)}, u32[]{:S(2)}) collective-permute-start(f32[768,640]{1,0:T(8,128)} %get-tuple-element.104), channel_id=1, source_target_pairs={{0,1},{1,0},{2,3},{3,2},{4,5},{5,4},{6,7},{7,6},{8,9},{9,8},{10,11... | collective-permute-start | bytes 5898248 | tf_op jit(solution)/shard_map/ppermute | solution.py:164
  171.4 25.6 %collective-permute-start.16 = (f32[320,2048]{1,0:T(8,128)}, f32[320,2048]{1,0:T(8,128)}, u32[]{:S(2)}, u32[]{:S(2)}) collective-permute-start(f32[320,2048]{1,0:T(8,128)} %constant_dynamic-slice_fusion.15), channel_id=1, source_target_pairs={{0,2},{2,0},{4,6},{6,4},{8,10},{10,8},{12,14},{14,12},{16,18},{18,... | collective-permute-start | bytes 7864328 | tf_op jit(solution)/shard_map/ppermute | solution.py:169
  171.4 30.2 %collective-permute-start.17 = (f32[320,2048]{1,0:T(8,128)}, f32[320,2048]{1,0:T(8,128)}, u32[]{:S(2)}, u32[]{:S(2)}) collective-permute-start(f32[320,2048]{1,0:T(8,128)} %constant_dynamic-slice_fusion.14), channel_id=1, source_target_pairs={{0,2},{2,0},{4,6},{6,4},{8,10},{10,8},{12,14},{14,12},{16,18},{18,... | collective-permute-start | bytes 7864328 | tf_op jit(solution)/shard_map/ppermute | solution.py:169
  184.6 16.9 %slice-start.4 = ((s8[5242880]{0:T(1024)(128)(4,1)}), s8[4194304]{0:T(1024)(128)(4,1)S(1)}, s32[]{:S(2)}) async-start(s8[5242880]{0:T(1024)(128)(4,1)} %bitcast.35), calls=%async_computation.4 | async-start | bytes 8388608
  232.2 55.3 %collective-permute-start.47 = (f32[160,2048]{1,0:T(8,128)}, f32[160,2048]{1,0:T(8,128)}, u32[]{:S(2)}, u32[]{:S(2)}) collective-permute-start(f32[160,2048]{1,0:T(8,128)} %constant_dynamic-slice_fusion), channel_id=1, source_target_pairs={{0,8},{2,10},{4,12},{6,14},{8,0},{10,2},{12,4},{14,6},{16,24},{18,... | collective-permute-start | bytes 3932168 | tf_op jit(solution)/shard_map/ppermute | solution.py:169
  234.9 56.4 %collective-permute-start.39 = (f32[160,2048]{1,0:T(8,128)}, f32[160,2048]{1,0:T(8,128)}, u32[]{:S(2)}, u32[]{:S(2)}) collective-permute-start(f32[160,2048]{1,0:T(8,128)} %constant_dynamic-slice_fusion.3), channel_id=1, source_target_pairs={{0,4},{2,6},{4,0},{6,2},{8,12},{10,14},{12,8},{14,10},{16,20},{18,... | collective-permute-start | bytes 3932168 | tf_op jit(solution)/shard_map/ppermute | solution.py:169
  238.5 36.1 %collective-permute-start.18 = (f32[768,512]{1,0:T(8,128)S(1)}, f32[768,512]{1,0:T(8,128)S(1)}, u32[]{:S(2)}, u32[]{:S(2)}) collective-permute-start(f32[768,512]{1,0:T(8,128)S(1)} %pad_maximum_fusion.11), channel_id=1, source_target_pairs={{0,1},{1,0},{2,3},{3,2},{4,5},{5,4},{6,7},{7,6},{8,9},{9,8},{10,11... | collective-permute-start | bytes 4718600 | tf_op jit(solution)/shard_map/ppermute | solution.py:164
  242.2 52.8 %collective-permute-start.30 = (f32[2,768,640]{2,1,0:T(8,128)}, f32[2,768,640]{2,1,0:T(8,128)}, u32[]{:S(2)}, u32[]{:S(2)}) collective-permute-start(f32[2,768,640]{2,1,0:T(8,128)} %constant_dynamic-slice_fusion.7), channel_id=1, source_target_pairs={{0,2},{2,0},{4,6},{6,4},{8,10},{10,8},{12,14},{14,12},{16,18},{18,... | collective-permute-start | bytes 11796488 | tf_op jit(solution)/shard_map/ppermute | solution.py:169
  287.4 11.1 %collective-permute-start.20 = (f32[328,1536]{1,0:T(8,128)S(1)}, f32[328,1536]{1,0:T(8,128)S(1)}, u32[]{:S(2)}, u32[]{:S(2)}) collective-permute-start(f32[328,1536]{1,0:T(8,128)S(1)} %constant_dynamic-slice_fusion.11), channel_id=1, source_target_pairs={{0,2},{2,0},{4,6},{6,4},{8,10},{10,8},{12,14},{14,12},{16,18},{18,... | collective-permute-start | bytes 6045704 | tf_op jit(solution)/shard_map/ppermute | solution.py:169
  290.7 17.8 %collective-permute-start.48 = (f32[160,1024]{1,0:T(8,128)S(1)}, f32[160,1024]{1,0:T(8,128)}, u32[]{:S(2)}, u32[]{:S(2)}) collective-permute-start(f32[160,1024]{1,0:T(8,128)S(1)} %slice.320), channel_id=1, source_target_pairs={{0,1},{1,0},{2,3},{3,2},{4,5},{5,4},{6,7},{7,6},{8,9},{9,8},{10,11... | collective-permute-start | bytes 1966088 | tf_op jit(solution)/shard_map/ppermute | solution.py:164
  293.0 29.5 %collective-permute-start.40 = (f32[160,1024]{1,0:T(8,128)S(1)}, f32[160,1024]{1,0:T(8,128)S(1)}, u32[]{:S(2)}, u32[]{:S(2)}) collective-permute-start(f32[160,1024]{1,0:T(8,128)S(1)} %slice.318), channel_id=1, source_target_pairs={{0,1},{1,0},{2,3},{3,2},{4,5},{5,4},{6,7},{7,6},{8,9},{9,8},{10,11... | collective-permute-start | bytes 1966088 | tf_op jit(solution)/shard_map/ppermute | solution.py:164
  295.0 192.9 %collective-permute-start.19 = (f32[768,640]{1,0:T(8,128)S(1)}, f32[768,640]{1,0:T(8,128)S(1)}, u32[]{:S(2)}, u32[]{:S(2)}) collective-permute-start(f32[768,640]{1,0:T(8,128)S(1)} %fusion.24), channel_id=1, source_target_pairs={{0,1},{1,0},{2,3},{3,2},{4,5},{5,4},{6,7},{7,6},{8,9},{9,8},{10,11... | collective-permute-start | bytes 5898248 | tf_op jit(solution)/shard_map/ppermute | solution.py:164
  298.5 49.3 %collective-permute-start.31 = (f32[2,384,640]{2,1,0:T(8,128)S(1)}, f32[2,384,640]{2,1,0:T(8,128)S(1)}, u32[]{:S(2)}, u32[]{:S(2)}) collective-permute-start(f32[2,384,640]{2,1,0:T(8,128)S(1)} %constant_dynamic-slice_fusion.6), channel_id=1, source_target_pairs={{0,8},{2,10},{4,12},{6,14},{8,0},{10,2},{12,4},{14,6},{16,24},{18,... | collective-permute-start | bytes 5898248 | tf_op jit(solution)/shard_map/ppermute | solution.py:169
  308.5 29.5 %collective-permute-start.21 = (f32[164,1536]{1,0:T(8,128)S(1)}, f32[164,1536]{1,0:T(8,128)S(1)}, u32[]{:S(2)}, u32[]{:S(2)}) collective-permute-start(f32[164,1536]{1,0:T(8,128)S(1)} %constant_dynamic-slice_fusion.10), channel_id=1, source_target_pairs={{0,4},{2,6},{4,0},{6,2},{8,12},{10,14},{12,8},{14,10},{16,20},{18,... | collective-permute-start | bytes 3022856 | tf_op jit(solution)/shard_map/ppermute | solution.py:169
  322.5 13.9 %collective-permute-start.49 = (f32[80,1024]{1,0:T(8,128)S(1)}, f32[80,1024]{1,0:T(8,128)S(1)}, u32[]{:S(2)}, u32[]{:S(2)}) collective-permute-start(f32[80,1024]{1,0:T(8,128)S(1)} %constant_dynamic-slice_fusion.22), channel_id=1, source_target_pairs={{0,4},{2,6},{4,0},{6,2},{8,12},{10,14},{12,8},{14,10},{16,20},{18,... | collective-permute-start | bytes 983048 | tf_op jit(solution)/shard_map/ppermute | solution.py:169
  336.3 15.7 %collective-permute-start.41 = (f32[80,1024]{1,0:T(8,128)S(1)}, f32[80,1024]{1,0:T(8,128)S(1)}, u32[]{:S(2)}, u32[]{:S(2)}) collective-permute-start(f32[80,1024]{1,0:T(8,128)S(1)} %constant_dynamic-slice_fusion.2), channel_id=1, source_target_pairs={{0,8},{2,10},{4,12},{6,14},{8,0},{10,2},{12,4},{14,6},{16,24},{18,... | collective-permute-start | bytes 983048 | tf_op jit(solution)/shard_map/ppermute | solution.py:169
  338.0 39.2 %collective-permute-start.50 = (f32[40,1024]{1,0:T(8,128)S(1)}, f32[40,1024]{1,0:T(8,128)S(1)}, u32[]{:S(2)}, u32[]{:S(2)}) collective-permute-start(f32[40,1024]{1,0:T(8,128)S(1)} %constant_dynamic-slice_fusion.23), channel_id=1, source_target_pairs={{0,16},{2,18},{4,20},{6,22},{8,24},{10,26},{12,28},{14,30},{16,0},... | collective-permute-start | bytes 491528 | tf_op jit(solution)/shard_map/ppermute | solution.py:169
  347.8 27.8 %collective-permute-start.22 = (f32[164,768]{1,0:T(8,128)S(1)}, f32[164,768]{1,0:T(8,128)S(1)}, u32[]{:S(2)}, u32[]{:S(2)}) collective-permute-start(f32[164,768]{1,0:T(8,128)S(1)} %slice.308), channel_id=1, source_target_pairs={{0,1},{1,0},{2,3},{3,2},{4,5},{5,4},{6,7},{7,6},{8,9},{9,8},{10,11... | collective-permute-start | bytes 1511432 | tf_op jit(solution)/shard_map/ppermute | solution.py:164
  352.0 42.7 %collective-permute-start.32 = (f32[384,640]{1,0:T(8,128)S(1)}, f32[384,640]{1,0:T(8,128)S(1)}, u32[]{:S(2)}, u32[]{:S(2)}) collective-permute-start(f32[384,640]{1,0:T(8,128)S(1)} %slice_bitcast_fusion), channel_id=1, source_target_pairs={{0,1},{1,0},{2,3},{3,2},{4,5},{5,4},{6,7},{7,6},{8,9},{9,8},{10,11... | collective-permute-start | bytes 2949128 | tf_op jit(solution)/shard_map/ppermute | solution.py:164
  375.8 8.9 %collective-permute-start.23 = (f32[82,768]{1,0:T(8,128)S(1)}, f32[82,768]{1,0:T(8,128)S(1)}, u32[]{:S(2)}, u32[]{:S(2)}) collective-permute-start(f32[82,768]{1,0:T(8,128)S(1)} %constant_dynamic-slice_fusion.9), channel_id=1, source_target_pairs={{0,8},{2,10},{4,12},{6,14},{8,0},{10,2},{12,4},{14,6},{16,24},{18,... | collective-permute-start | bytes 755720 | tf_op jit(solution)/shard_map/ppermute | solution.py:169
  377.2 19.0 %collective-permute-start.42 = (f32[40,1024]{1,0:T(8,128)S(1)}, f32[40,1024]{1,0:T(8,128)S(1)}, u32[]{:S(2)}, u32[]{:S(2)}) collective-permute-start(f32[40,1024]{1,0:T(8,128)S(1)} %constant_dynamic-slice_fusion.1), channel_id=1, source_target_pairs={{0,16},{2,18},{4,20},{6,22},{8,24},{10,26},{12,28},{14,30},{16,0},... | collective-permute-start | bytes 491528 | tf_op jit(solution)/shard_map/ppermute | solution.py:169
  384.7 35.4 %collective-permute-start.51 = (f32[40,1024]{1,0:T(8,128)S(1)}, f32[40,1024]{1,0:T(8,128)S(1)}, u32[]{:S(2)}, u32[]{:S(2)}) collective-permute-start(f32[40,1024]{1,0:T(8,128)S(1)} %dynamic-slice_add_fusion.13), channel_id=1, source_target_pairs={{0,16},{2,18},{4,20},{6,22},{8,24},{10,26},{12,28},{14,30},{16,0},... | collective-permute-start | bytes 491528 | tf_op jit(solution)/shard_map/ppermute | solution.py:169
  394.9 11.3 %collective-permute-start.33 = (f32[192,640]{1,0:T(8,128)S(1)}, f32[192,640]{1,0:T(8,128)S(1)}, u32[]{:S(2)}, u32[]{:S(2)}) collective-permute-start(f32[192,640]{1,0:T(8,128)S(1)} %constant_dynamic-slice_fusion.5), channel_id=1, source_target_pairs={{0,4},{2,6},{4,0},{6,2},{8,12},{10,14},{12,8},{14,10},{16,20},{18,... | collective-permute-start | bytes 1474568 | tf_op jit(solution)/shard_map/ppermute | solution.py:169
  396.2 7.7 %collective-permute-start.24 = (f32[41,768]{1,0:T(8,128)S(1)}, f32[41,768]{1,0:T(8,128)S(1)}, u32[]{:S(2)}, u32[]{:S(2)}) collective-permute-start(f32[41,768]{1,0:T(8,128)S(1)} %constant_dynamic-slice_fusion.8), channel_id=1, source_target_pairs={{0,16},{2,18},{4,20},{6,22},{8,24},{10,26},{12,28},{14,30},{16,0},... | collective-permute-start | bytes 377864 | tf_op jit(solution)/shard_map/ppermute | solution.py:169
  404.0 18.9 %collective-permute-start.43 = (f32[40,1024]{1,0:T(8,128)S(1)}, f32[40,1024]{1,0:T(8,128)S(1)}, u32[]{:S(2)}, u32[]{:S(2)}) collective-permute-start(f32[40,1024]{1,0:T(8,128)S(1)} %dynamic-slice_add_fusion.14), channel_id=1, source_target_pairs={{0,16},{2,18},{4,20},{6,22},{8,24},{10,26},{12,28},{14,30},{16,0},... | collective-permute-start | bytes 491528 | tf_op jit(solution)/shard_map/ppermute | solution.py:169
  406.2 4.1 collective-permute-start.25
  410.2 9.6 %collective-permute-start.34 = (f32[96,640]{1,0:T(8,128)S(1)}, f32[96,640]{1,0:T(8,128)S(1)}, u32[]{:S(2)}, u32[]{:S(2)}) collective-permute-start(f32[96,640]{1,0:T(8,128)S(1)} %constant_dynamic-slice_fusion.4), channel_id=1, source_target_pairs={{0,16},{2,18},{4,20},{6,22},{8,24},{10,26},{12,28},{14,30},{16,0},... | collective-permute-start | bytes 737288 | tf_op jit(solution)/shard_map/ppermute | solution.py:169
  419.8 12.9 %collective-permute-start.26 = (f32[41,1024]{1,0:T(8,128)S(1)}, f32[41,1024]{1,0:T(8,128)S(1)}, u32[]{:S(2)}, u32[]{:S(2)}) collective-permute-start(f32[41,1024]{1,0:T(8,128)S(1)} %pad_maximum_fusion.33), channel_id=1, source_target_pairs={{0,16},{2,18},{4,20},{6,22},{8,24},{10,26},{12,28},{14,30},{16,0},... | collective-permute-start | bytes 503816 | tf_op jit(solution)/shard_map/ppermute | solution.py:169
  420.1 23.2 %collective-permute-start.35 = (f32[96,640]{1,0:T(8,128)S(1)}, f32[96,640]{1,0:T(8,128)S(1)}, u32[]{:S(2)}, u32[]{:S(2)}) collective-permute-start(f32[96,640]{1,0:T(8,128)S(1)} %dynamic-slice_add_fusion.12), channel_id=1, source_target_pairs={{0,16},{2,18},{4,20},{6,22},{8,24},{10,26},{12,28},{14,30},{16,0},... | collective-permute-start | bytes 737288 | tf_op jit(solution)/shard_map/ppermute | solution.py:169
  422.9 27.4 %collective-permute-start.52 = (f32[80,1024]{1,0:T(8,128)S(1)}, f32[80,1024]{1,0:T(8,128)S(1)}, u32[]{:S(2)}, u32[]{:S(2)}) collective-permute-start(f32[80,1024]{1,0:T(8,128)S(1)} %maximum_select_fusion.27), channel_id=1, source_target_pairs={{0,4},{2,6},{4,0},{6,2},{8,12},{10,14},{12,8},{14,10},{16,20},{18,... | collective-permute-start | bytes 983048 | tf_op jit(solution)/shard_map/ppermute | solution.py:169
  432.8 19.0 %collective-permute-start.44 = (f32[80,1024]{1,0:T(8,128)S(1)}, f32[80,1024]{1,0:T(8,128)S(1)}, u32[]{:S(2)}, u32[]{:S(2)}) collective-permute-start(f32[80,1024]{1,0:T(8,128)S(1)} %maximum_select_fusion.26), channel_id=1, source_target_pairs={{0,8},{2,10},{4,12},{6,14},{8,0},{10,2},{12,4},{14,6},{16,24},{18,... | collective-permute-start | bytes 983048 | tf_op jit(solution)/shard_map/ppermute | solution.py:169
  443.2 16.3 %collective-permute-start.27 = (f32[82,1024]{1,0:T(8,128)S(1)}, f32[82,1024]{1,0:T(8,128)S(1)}, u32[]{:S(2)}, u32[]{:S(2)}) collective-permute-start(f32[82,1024]{1,0:T(8,128)S(1)} %maximum_select_fusion.25), channel_id=1, source_target_pairs={{0,8},{2,10},{4,12},{6,14},{8,0},{10,2},{12,4},{14,6},{16,24},{18,... | collective-permute-start | bytes 1007624 | tf_op jit(solution)/shard_map/ppermute | solution.py:169
  448.5 14.2 %collective-permute-start.36 = (f32[192,640]{1,0:T(8,128)S(1)}, f32[192,640]{1,0:T(8,128)S(1)}, u32[]{:S(2)}, u32[]{:S(2)}) collective-permute-start(f32[192,640]{1,0:T(8,128)S(1)} %maximum_select_fusion.24), channel_id=1, source_target_pairs={{0,4},{2,6},{4,0},{6,2},{8,12},{10,14},{12,8},{14,10},{16,20},{18,... | collective-permute-start | bytes 1474568 | tf_op jit(solution)/shard_map/ppermute | solution.py:169
  450.4 23.2 %collective-permute-start.53 = (f32[160,1024]{1,0:T(8,128)S(1)}, f32[160,1024]{1,0:T(8,128)S(1)}, u32[]{:S(2)}, u32[]{:S(2)}) collective-permute-start(f32[160,1024]{1,0:T(8,128)S(1)} %maximum_select_fusion.23), channel_id=1, source_target_pairs={{0,8},{2,10},{4,12},{6,14},{8,0},{10,2},{12,4},{14,6},{16,24},{18,... | collective-permute-start | bytes 1966088 | tf_op jit(solution)/shard_map/ppermute | solution.py:169
  451.9 21.9 %collective-permute-start.45 = (f32[160,1024]{1,0:T(8,128)S(1)}, f32[160,1024]{1,0:T(8,128)S(1)}, u32[]{:S(2)}, u32[]{:S(2)}) collective-permute-start(f32[160,1024]{1,0:T(8,128)S(1)} %maximum_select_fusion.22), channel_id=1, source_target_pairs={{0,4},{2,6},{4,0},{6,2},{8,12},{10,14},{12,8},{14,10},{16,20},{18,... | collective-permute-start | bytes 1966088 | tf_op jit(solution)/shard_map/ppermute | solution.py:169
  459.6 20.2 %collective-permute-start.28 = (f32[164,1024]{1,0:T(8,128)S(1)}, f32[164,1024]{1,0:T(8,128)S(1)}, u32[]{:S(2)}, u32[]{:S(2)}) collective-permute-start(f32[164,1024]{1,0:T(8,128)S(1)} %maximum_select_fusion.19), channel_id=1, source_target_pairs={{0,4},{2,6},{4,0},{6,2},{8,12},{10,14},{12,8},{14,10},{16,20},{18,... | collective-permute-start | bytes 2015240 | tf_op jit(solution)/shard_map/ppermute | solution.py:169
  462.8 24.9 %collective-permute-start.37 = (f32[384,640]{1,0:T(8,128)S(1)}, f32[384,640]{1,0:T(8,128)S(1)}, u32[]{:S(2)}, u32[]{:S(2)}) collective-permute-start(f32[384,640]{1,0:T(8,128)S(1)} %maximum_select_fusion.18), channel_id=1, source_target_pairs={{0,8},{2,10},{4,12},{6,14},{8,0},{10,2},{12,4},{14,6},{16,24},{18,... | collective-permute-start | bytes 2949128 | tf_op jit(solution)/shard_map/ppermute | solution.py:169
  473.7 16.7 %collective-permute-start.54 = (f32[320,1024]{1,0:T(8,128)S(1)}, f32[320,1024]{1,0:T(8,128)}, u32[]{:S(2)}, u32[]{:S(2)}) collective-permute-start(f32[320,1024]{1,0:T(8,128)S(1)} %maximum_select_fusion.17), channel_id=1, source_target_pairs={{0,2},{2,0},{4,6},{6,4},{8,10},{10,8},{12,14},{14,12},{16,18},{18,... | collective-permute-start | bytes 3932168 | tf_op jit(solution)/shard_map/ppermute | solution.py:169
  474.0 20.1 %collective-permute-start.46 = (f32[320,1024]{1,0:T(8,128)S(1)}, f32[320,1024]{1,0:T(8,128)}, u32[]{:S(2)}, u32[]{:S(2)}) collective-permute-start(f32[320,1024]{1,0:T(8,128)S(1)} %maximum_select_fusion.16), channel_id=1, source_target_pairs={{0,2},{2,0},{4,6},{6,4},{8,10},{10,8},{12,14},{14,12},{16,18},{18,... | collective-permute-start | bytes 3932168 | tf_op jit(solution)/shard_map/ppermute | solution.py:169
  480.1 17.8 %collective-permute-start.29 = (f32[328,1024]{1,0:T(8,128)S(1)}, f32[328,1024]{1,0:T(8,128)S(1)}, u32[]{:S(2)}, u32[]{:S(2)}) collective-permute-start(f32[328,1024]{1,0:T(8,128)S(1)} %maximum_select_fusion.10), channel_id=1, source_target_pairs={{0,2},{2,0},{4,6},{6,4},{8,10},{10,8},{12,14},{14,12},{16,18},{18,... | collective-permute-start | bytes 4030472 | tf_op jit(solution)/shard_map/ppermute | solution.py:169
  487.8 13.9 %collective-permute-start.38 = (f32[768,640]{1,0:T(8,128)S(1)}, f32[768,640]{1,0:T(8,128)S(1)}, u32[]{:S(2)}, u32[]{:S(2)}) collective-permute-start(f32[768,640]{1,0:T(8,128)S(1)} %maximum_select_fusion.9), channel_id=1, source_target_pairs={{0,2},{2,0},{4,6},{6,4},{8,10},{10,8},{12,14},{14,12},{16,18},{18,... | collective-permute-start | bytes 5898248 | tf_op jit(solution)/shard_map/ppermute | solution.py:169
  (61 other events, 238.6 us)
